TPU v7x, 512 devices: a whole 4x8x8 slice. The times are simulated.
512 devices in a mesh: row: 8 (over y), col: 64 (over z, x, core).
Axes of the slice: x: 4, y: 8, z: 8, core: 2. Of those that a mesh axis runs over, the one named last changes fastest.
Arguments:
- sigma_top: bfloat16 [16384, 8, 64, 32], P('row', None, 'col'), as said below
- ancestor_rows: float32 [16384, 1024], P(('row', 'col')), may hold values from -0.0009765625 to 0.0009765625
- window_rows: float32 [1024, 1024], P('col'), may hold values from -0.1875 to 0.1875
- tile_inverse: float32 [4, 256, 256], replicated, as said below
- structure: int32 [4, 64], replicated, may hold values from 0 to 1, as said below
Outputs:
- cross_covariance: float32 [16384, 1024], P(('row', 'col'))
- window_covariance: float32 [1024, 1024], P('col')
Inputs may be any that keep to these rules, and one draw needn't show every extreme that they name: `sigma_top`: symmetric as an 16384 x 16384 matrix. `tile_inverse`: each tile is lower triangular. A tile in the structure of supernode j lies in the structure of every earlier supernode; supernode 0's structure holds every ancestor tile.
All inputs are finite; a program needn't handle non-finite values.
Results may differ from a plain program's by a relative error of at most 0.0013.
The roundings to bfloat16 on the way count: a program that leaves them out, or rounds other values in their place, can miss the bound.
Values may be sent and summed in bfloat16 or wider, within the bound.
No kernel may reach another device: no remote copies, remote signals or barrier semaphores. Data moves between devices by JAX's collectives and lax.ppermute only.
A program may use at most 64 MiB of HBM per device.

v0:
```python
import jax
import jax.numpy as jnp
from jax import lax
from jax.sharding import PartitionSpec as P


def lookup_rows(flags, tiles):
    matches = tiles[:, None] == jnp.arange(flags.shape[0], dtype=jnp.int32)[None, :]
    return jnp.sum(jnp.where(matches, flags[None, :], 0), axis=1).astype(jnp.float32)


def diagonal_total(partial_value):
    return lax.psum(partial_value, ("row", "col"))


def body(sigma_top, ancestor_rows, window_rows, tile_inverse, structure):
    highest = lax.Precision.HIGHEST
    supernodes = tile_inverse.shape[0]
    tile_width = tile_inverse.shape[1]
    window = supernodes * tile_width
    block_rows = sigma_top.shape[0]
    row_groups = sigma_top.shape[1]
    local_rows = ancestor_rows.shape[0]
    window_local = window_rows.shape[0]
    device_flat = lax.axis_index(("row", "col"))
    column_index = lax.axis_index("col")
    row_index = lax.axis_index("row")
    tiles_ancestor = (
        device_flat * local_rows + jnp.arange(local_rows, dtype=jnp.int32)
    ) // tile_width
    tiles_window = (
        column_index * window_local + jnp.arange(window_local, dtype=jnp.int32)
    ) // tile_width
    column_tiles = jnp.arange(window, dtype=jnp.int32) // tile_width
    upper_mask = column_tiles[None, :] > tiles_window[:, None]
    sigma_flat = sigma_top.reshape(block_rows, row_groups * local_rows)
    first_row = (row_index == 0).astype(jnp.float32)
    selections = [
        lookup_rows(structure[supernode], tiles_ancestor) for supernode in range(supernodes)
    ]
    cross = jnp.zeros((local_rows, window), jnp.float32)
    block = jnp.zeros((window_local, window), jnp.float32)
    for supernode in range(supernodes):
        left_edge = supernode * tile_width
        right_edge = left_edge + tile_width
        panel_product = jnp.dot(
            ancestor_rows[:, supernode * tile_width : (supernode + 1) * tile_width],
            tile_inverse[supernode],
            precision=highest,
            preferred_element_type=jnp.float32,
        )
        panel_anc = (selections[supernode][:, None] * panel_product).astype(jnp.bfloat16)
        keep = (tiles_window < supernode).astype(jnp.float32)
        product = jnp.dot(
            window_rows[:, supernode * tile_width : (supernode + 1) * tile_width],
            tile_inverse[supernode],
            precision=highest,
            preferred_element_type=jnp.float32,
        )
        panel_own = (keep[:, None] * product).astype(jnp.bfloat16)
        folded = lax.dot_general(
            sigma_flat,
            lax.all_gather(panel_anc, "col", axis=0, tiled=True),
            (((0,), (0,)), ((), ())),
            preferred_element_type=jnp.float32,
        )
        ancestor_part = lax.psum_scatter(
            folded.reshape(row_groups, local_rows, tile_width),
            "row",
            scatter_dimension=0,
            tiled=True,
        ).reshape(local_rows, tile_width)
        panel_all = lax.all_gather(panel_own, "col", axis=0, tiled=True)
        ancestor_f32 = panel_anc.astype(jnp.float32)
        own_f32 = panel_own.astype(jnp.float32)
        window_f32 = panel_all.astype(jnp.float32)
        result_ancestor = selections[supernode][:, None] * (
            ancestor_part
            + jnp.dot(cross, window_f32, precision=highest, preferred_element_type=jnp.float32)
        )
        diagonal_term = jnp.dot(
            ancestor_f32.T, result_ancestor, precision=highest, preferred_element_type=jnp.float32
        )
        if supernode > 0:
            upper = jnp.where(upper_mask, block, 0.0)
            upper_term = jnp.dot(
                upper, window_f32, precision=highest, preferred_element_type=jnp.float32
            )
            placed_term = lax.dynamic_update_slice_in_dim(
                jnp.zeros((window, tile_width), jnp.float32),
                upper_term,
                column_index * window_local,
                0,
            )
            window_term = jnp.dot(
                cross.T, ancestor_f32, precision=highest, preferred_element_type=jnp.float32
            )
            window_term = window_term + first_row * (
                jnp.dot(block.T, own_f32, precision=highest, preferred_element_type=jnp.float32)
                + placed_term
            )
            window_term = window_term[:left_edge]
            window_sum = lax.psum(window_term, ("row", "col"))
            diagonal_sum = diagonal_total(diagonal_term)
            result_window = jnp.concatenate(
                [window_sum, jnp.zeros((window - left_edge, tile_width), jnp.float32)], axis=0
            )
            window_part = jnp.dot(
                window_f32.T, result_window, precision=highest, preferred_element_type=jnp.float32
            )
            mine_result = lax.dynamic_slice_in_dim(
                result_window, column_index * window_local, window_local, 0
            )
        else:
            mine_result = jnp.zeros((window_local, tile_width), jnp.float32)
            window_part = jnp.zeros((tile_width, tile_width), jnp.float32)
            diagonal_sum = diagonal_total(diagonal_term)
        inverse = tile_inverse[supernode]
        diagonal = jnp.dot(
            inverse.T, inverse, precision=highest, preferred_element_type=jnp.float32
        )
        diagonal = diagonal + window_part + diagonal_sum
        placed = jnp.zeros((window, tile_width), jnp.float32).at[left_edge:right_edge].set(diagonal)
        mine_diagonal = lax.dynamic_slice_in_dim(
            placed, column_index * window_local, window_local, 0
        )
        row_tiles = tiles_window[:, None]
        column = jnp.where(
            row_tiles < supernode,
            -mine_result,
            jnp.where(row_tiles == supernode, mine_diagonal, 0.0),
        )
        cross = cross.at[:, left_edge:right_edge].set(-result_ancestor)
        block = block.at[:, left_edge:right_edge].set(column)
    return (cross, block)


def solution(mesh):
    placed = (P("row", None, "col", None), P(("row", "col"), None), P("col", None), P(), P())
    return jax.shard_map(
        body,
        mesh=mesh,
        in_specs=placed,
        out_specs=(P(("row", "col"), None), P("col", None)),
        check_vma=False,
    )
```

profile of v0, /device:TPU:23, one launch (start us, length us, event | category | flops | bytes accessed | tf_op | source)
XLA Modules:
  0.0 1614.0 jit_solution(3560617816976950300)
XLA Ops:
  7.3 0.7 copy-done.16
  8.2 1.8 fusion.22
  10.2 1.8 fusion.23
  12.1 1.8 fusion.24
  13.9 84.5 %all-gather.5.cloned.1.call-done = bf16[2048,256]{1,0:T(8,128)(2,1)} async-done(((bf16[32,256]{1,0:T(8,128)(2,1)}), bf16[2048,256]{1,0:T(8,128)(2,1)}) %all-gather.5.cloned.1.call-update) | async-done | bytes 1048592 | tf_op jit(solution)/shard_map/all_gather | solution.py:63
  98.5 2.5 fusion.111
  101.0 0.8 fusion.25
  102.3 52.7 %all_gather.25 = bf16[1024,256]{1,0:T(8,128)(2,1)} all-gather(bf16[16,256]{1,0:T(8,128)(2,1)S(1)} %fusion.29), channel_id=1, replica_groups=mesh['row'=8,'col'=64] {'col'}, dimensions={0}, use_global_device_ids=true | all-gather | bytes 532480 | tf_op jit(solution)/shard_map/all_gather | solution.py:73
  155.3 49.1 %all_gather.27 = bf16[1024,256]{1,0:T(8,128)(2,1)S(1)} all-gather(bf16[16,256]{1,0:T(8,128)(2,1)S(1)} %fusion.30), channel_id=1, replica_groups=mesh['row'=8,'col'=64] {'col'}, dimensions={0}, use_global_device_ids=true | all-gather | bytes 532480 | tf_op jit(solution)/shard_map/all_gather | solution.py:73
  204.6 48.0 %all_gather.29 = bf16[1024,256]{1,0:T(8,128)(2,1)S(1)} all-gather(bf16[16,256]{1,0:T(8,128)(2,1)S(1)} %fusion.31), channel_id=1, replica_groups=mesh['row'=8,'col'=64] {'col'}, dimensions={0}, use_global_device_ids=true | all-gather | bytes 532480 | tf_op jit(solution)/shard_map/all_gather | solution.py:73
  252.8 54.0 %all_gather.31 = bf16[1024,256]{1,0:T(8,128)(2,1)} all-gather(bf16[16,256]{1,0:T(8,128)(2,1)S(1)} %fusion.32), channel_id=1, replica_groups=mesh['row'=8,'col'=64] {'col'}, dimensions={0}, use_global_device_ids=true | all-gather | bytes 532480 | tf_op jit(solution)/shard_map/all_gather | solution.py:73
  306.9 1.3 fusion.41
  308.2 2.4 fusion.112
  310.7 1.3 fusion.37
  312.0 2.4 fusion.113
  314.4 0.7 compare_reduce_fusion.2
  315.1 0.7 compare_reduce_fusion.1
  315.8 0.7 compare_reduce_fusion
  316.4 2.1 negate_select_fusion
  318.5 1.0 fusion.103
  319.6 70.1 %all-gather.11.cloned.1.call-done = bf16[2048,256]{1,0:T(8,128)(2,1)} async-done(((bf16[32,256]{1,0:T(8,128)(2,1)}), bf16[2048,256]{1,0:T(8,128)(2,1)}) %all-gather.11.cloned.1.call-update) | async-done | bytes 1048592 | tf_op jit(solution)/shard_map/all_gather | solution.py:63
  389.7 2.4 fusion.114
  392.8 1.6 fusion.60
  394.4 28.6 %reduce-scatter.7.cloned.1.call-done = f32[1,32,256]{2,1,0:T(8,128)} async-done(((f32[8,32,256]{2,1,0:T(8,128)}), f32[1,32,256]{2,1,0:T(8,128)}) %reduce-scatter.7.cloned.1.call-update) | async-done | bytes 32784 | tf_op jit(solution)/shard_map/reduce_scatter | solution.py:67
  422.9 1.7 select_dynamic-update-slice_fusion
  424.7 1.0 fusion.104
  425.7 1.6 fusion.105
  427.3 36.5 %reduce-scatter.9.cloned.1.call-done = f32[1,32,256]{2,1,0:T(8,128)} async-done(((f32[8,32,256]{2,1,0:T(8,128)}), f32[1,32,256]{2,1,0:T(8,128)}) %reduce-scatter.9.cloned.1.call-update) | async-done | bytes 32784 | tf_op jit(solution)/shard_map/reduce_scatter | solution.py:67
  463.8 1.1 fusion.19
  465.0 1.0 fusion.107
  466.0 277.6 %all-reduce.17.cloned.1.call-done = f32[256,256]{1,0:T(8,128)} async-done(((f32[256,256]{1,0:T(8,128)}), f32[256,256]{1,0:T(8,128)}) %all-reduce.17.cloned.1.call-update) | async-done | bytes 262160 | tf_op jit(solution)/shard_map/psum | solution.py:13
  743.6 1.5 convolution_add_fusion.1
  745.1 0.7 select_select_fusion
  746.8 1.7 slice_add_fusion.2
  749.2 25.0 %reduce-scatter.11.cloned.1.call-done = f32[1,32,256]{2,1,0:T(8,128)} async-done(((f32[8,32,256]{2,1,0:T(8,128)}), f32[1,32,256]{2,1,0:T(8,128)}) %reduce-scatter.11.cloned.1.call-update) | async-done | bytes 32784 | tf_op jit(solution)/shard_map/reduce_scatter | solution.py:67
  774.2 1.4 fusion.18
  775.6 281.1 %all-reduce.23.cloned.1.call-done = (f32[256,256]{1,0:T(8,128)}, f32[256,256]{1,0:T(8,128)}) async-done(((f32[256,256]{1,0:T(8,128)}, f32[256,256]{1,0:T(8,128)}), (f32[256,256]{1,0:T(8,128)}, f32[256,256]{1,0:T(8,128)})) %all-reduce.23.cloned.1.call-update) | async-done | bytes 524304 | tf_op jit(solution)/shard_map/psum | solution.py:13
  1056.7 1.8 fusion.13
  1058.5 0.8 select_dynamic-update-slice_fusion.2
  1060.3 0.9 slice_add_fusion.1
  1061.9 1.0 fusion.110
  1063.0 1.6 fusion.108
  1064.6 265.4 %all-reduce.21.cloned.1.call-done = (f32[256,256]{1,0:T(8,128)}, f32[512,256]{1,0:T(8,128)}) async-done(((f32[256,256]{1,0:T(8,128)}, f32[512,256]{1,0:T(8,128)}), (f32[256,256]{1,0:T(8,128)}, f32[512,256]{1,0:T(8,128)})) %all-reduce.21.cloned.1.call-update) | async-done | bytes 786448 | tf_op jit(solution)/shard_map/psum | solution.py:13
  1330.0 2.0 fusion.7
  1332.0 0.7 fusion.81
  1334.1 1.0 slice_add_fusion
  1335.8 268.6 %all-reduce.19.cloned.1.call-done = (f32[256,256]{1,0:T(8,128)}, f32[768,256]{1,0:T(8,128)}) async-done(((f32[256,256]{1,0:T(8,128)}, f32[768,256]{1,0:T(8,128)}), (f32[256,256]{1,0:T(8,128)}, f32[768,256]{1,0:T(8,128)})) %all-reduce.19.cloned.1.call-update) | async-done | bytes 1048592 | tf_op jit(solution)/shard_map/psum | solution.py:13
  1604.4 2.0 fusion.16
  (93 shorter events, 8.5 us)
Async XLA Ops:
  7.2 91.3 %copy-start = (bf16[2048,8,1,32]{0,3,2,1:T(8,128)(2,1)S(1)}, bf16[2048,8,1,32]{0,3,2,1:T(8,128)(2,1)}, u32[]{:S(2)}) copy-start(bf16[2048,8,1,32]{0,3,2,1:T(8,128)(2,1)} %param.29) | copy-start | bytes 3145732
  7.2 91.3 %all-gather.5.cloned.1.call-start = ((), (), s32[]{:S(2)}) async-start(), calls=%async_computation.4 | async-start | bytes 1064960 | tf_op jit(solution)/shard_map/all_gather | solution.py:63
  7.2 0.8 copy-start.16
  8.2 1.9 copy-start.14
  10.1 298.1 %all-gather.7.cloned.1.call-start = ((), (), s32[]{:S(2)}) async-start(), calls=%async_computation.6 | async-start | bytes 1064960 | tf_op jit(solution)/shard_map/all_gather | solution.py:63
  12.0 300.0 %all-gather.9.cloned.1.call-start = ((), (), s32[]{:S(2)}) async-start(), calls=%async_computation.8 | async-start | bytes 1064960 | tf_op jit(solution)/shard_map/all_gather | solution.py:63
  13.9 302.6 %reduce-scatter.5.cloned.1.call-start = ((), (), s32[]{:S(2)}) async-start(), calls=%async_computation.5 | async-start | bytes 294912 | tf_op jit(solution)/shard_map/reduce_scatter | solution.py:67
  98.5 2.6 copy-start.1
  101.0 288.7 %all-gather.11.cloned.1.call-start = ((), (), s32[]{:S(2)}) async-start(), calls=%async_computation.10 | async-start | bytes 1064960 | tf_op jit(solution)/shard_map/all_gather | solution.py:63
  101.0 1.0 copy-start.15
  101.9 321.0 %reduce-scatter.7.cloned.1.call-start = ((), (), s32[]{:S(2)}) async-start(), calls=%async_computation.7 | async-start | bytes 294912 | tf_op jit(solution)/shard_map/reduce_scatter | solution.py:67
  310.6 153.2 %reduce-scatter.9.cloned.1.call-start = ((), (), s32[]{:S(2)}) async-start(), calls=%async_computation.9 | async-start | bytes 294912 | tf_op jit(solution)/shard_map/reduce_scatter | solution.py:67
  314.4 429.2 %all-reduce.17.cloned.1.call-start = ((), (), s32[]{:S(2)}) async-start(), calls=%async_computation.12 | async-start | bytes 524288 | tf_op jit(solution)/shard_map/psum | solution.py:13
  316.4 2.1 copy-start.13
  319.6 454.6 %reduce-scatter.11.cloned.1.call-start = ((), (), s32[]{:S(2)}) async-start(), calls=%async_computation.11 | async-start | bytes 294912 | tf_op jit(solution)/shard_map/reduce_scatter | solution.py:67
  392.0 0.7 copy-start.11
  392.1 664.6 %all-reduce.23.cloned.1.call-start = ((), (), s32[]{:S(2)}) async-start(), calls=%async_computation.15 | async-start | bytes 1048576 | tf_op jit(solution)/shard_map/psum | solution.py:13
  424.7 1.1 copy-start.12
  748.5 581.4 %all-reduce.21.cloned.1.call-start = ((), (), s32[]{:S(2)}) async-start(), calls=%async_computation.14 | async-start | bytes 1572864 | tf_op jit(solution)/shard_map/psum | solution.py:13
  1056.7 1.8 copy-start.9
  1058.5 1.8 copy-start.6
  1061.2 0.7 copy-start.10
  1061.3 543.2 %all-reduce.19.cloned.1.call-start = ((), (), s32[]{:S(2)}) async-start(), calls=%async_computation.13 | async-start | bytes 2097152 | tf_op jit(solution)/shard_map/psum | solution.py:13
  1330.0 2.0 copy-start.7
  1332.7 1.0 copy-start.2
  1332.7 1.4 copy-start.4
  1335.8 270.7 %copy-start.3 = (f32[32,1024]{1,0:T(8,128)}, f32[32,1024]{1,0:T(8,128)S(1)}, u32[]{:S(2)}) copy-start(f32[32,1024]{1,0:T(8,128)S(1)} %negate_dynamic-update-slice_fusion) | copy-start | bytes 393220
  1604.4 2.0 copy-start.5
  1606.5 0.6 copy-start.8
Sparse Core Ops, SparseCore 0:
  11.9 86.4 all-gather.4
  102.4 79.7 all-gather.6
  185.5 79.7 all-gather.8
  268.0 30.7 reduce-scatter.4
  302.6 87.0 all-gather.10
  392.5 30.3 reduce-scatter.6
  425.7 38.0 reduce-scatter.8
  469.6 273.9 all-reduce.16
  746.4 27.7 reduce-scatter.10
  780.1 276.5 all-reduce.22
  1061.9 268.0 all-reduce.20
  1335.3 269.0 all-reduce.18
where the time goes:
time: 1610 us
  waiting for transfers between devices  1340 us (83%)
  blocking collectives  204 us (13%)
  matrix products  45.4 us (3%)
    psum x4, waiting for transfers between devices, diagonal_total(): return lax.psum(partial_value, ('row', 'col'))  1090 us
    all_gather x4, blocking collectives, body(): panel_all = lax.all_gather(panel_own, 'col', axis=0, tiled=True)  204 us
    all_gather x4, waiting for transfers between devices, body(): lax.all_gather(panel_anc, 'col', axis=0, tiled=True)  155 us
    reduce_scatter x4, waiting for transfers between devices, body(): lax.psum_scatter(folded.reshape(row_groups, local_rows, tile_width), 'row...  90 us
  transfers between devices with their start and end apart: 12, of which 9 were waited for; matrix products, arithmetic and copies ran while one was open for 3% of the time, Pallas kernels for 0%

commit v1 on v0

v1 whole, which is shorter than its diff:
```python
import jax
import jax.numpy as jnp
from jax import lax
from jax.sharding import Mesh, PartitionSpec as P

HIGHEST = lax.Precision.HIGHEST
HIGH = lax.Precision.HIGH
BF16 = jnp.bfloat16
F32 = jnp.float32


def mm(a, b, precision=HIGH):
    return jnp.dot(a, b, precision=precision, preferred_element_type=F32)


def mm_t(a, b, precision=HIGH):
    return lax.dot_general(
        a, b, (((0,), (0,)), ((), ())), precision=precision, preferred_element_type=F32
    )


def exchange(x, axis):
    return lax.all_to_all(x, axis, 0, 0, tiled=True)


def gather(x, axis, size):
    return exchange(jnp.broadcast_to(x[None], (size,) + x.shape), axis)


def body(sigma_top, ancestor_rows, window_rows, tile_inverse, structure):
    ny, nz, nx, nc = 8, 8, 4, 2
    supernodes, width = tile_inverse.shape[0], tile_inverse.shape[1]
    window = supernodes * width
    local = ancestor_rows.shape[0]
    wlocal = window_rows.shape[0]
    y, z, x, c = (lax.axis_index(name) for name in ("y", "z", "x", "c"))
    col = (z * nx + x) * nc + c
    tile = ((y * (nz * nx * nc) + col) * local) // width
    wtile = (col * wlocal) // width
    select = lax.dynamic_slice_in_dim(structure, tile, 1, 1)[:, 0].astype(F32)

    with jax.named_scope("panels"):
        rows = jnp.concatenate([ancestor_rows, window_rows], axis=0)
        pieces = [
            mm(rows[:, j * width : (j + 1) * width], tile_inverse[j], HIGHEST)
            for j in range(supernodes)
        ]
        panel = jnp.concatenate(
            [(select[j] * pieces[j][:local]).astype(BF16) for j in range(supernodes)], axis=1
        )
        wpanel = jnp.concatenate(
            [
                ((wtile < j).astype(F32) * pieces[j][local:]).astype(BF16)
                for j in range(1, supernodes)
            ],
            axis=1,
        )
        half = window - width
        folded = jnp.concatenate([wpanel[:, : half // 2], wpanel[:, half // 2 :]], axis=0)
        message = jnp.concatenate([panel, folded], axis=1)

    with jax.named_scope("column_block"):
        doubled = jnp.concatenate([panel, panel], axis=1)
        panel_c = lax.all_gather(doubled, "y", axis=0, tiled=True)[:, :window]

    with jax.named_scope("sigma"):
        sigma = sigma_top.reshape(nz, nx, nc, local, ny * local)
        mine = lax.dynamic_index_in_dim(sigma, c, 2, keepdims=False)
        other = lax.dynamic_index_in_dim(sigma, 1 - c, 2, keepdims=False)
        mine = mine.transpose(1, 0, 2, 3).reshape(-1, ny * local)
        other = other.transpose(1, 0, 2, 3).reshape(-1, ny * local)

    with jax.named_scope("gather"):
        got = gather(message, "z", nz).reshape(nz * local, -1)
        got = gather(got, "x", nx).reshape(nx * nz * local, -1)
        sibling = lax.ppermute(got, "c", [(0, 1), (1, 0)])
        product = mm_t(mine, got[:, :window], None) + mm_t(other, sibling[:, :window], None)

    with jax.named_scope("unit_inverse"):
        swap = c == 1
        w_mine, w_other = (
            v[:, window:].reshape(nx, nz, 2, wlocal, half // 2) for v in (got, sibling)
        )
        w_all = jnp.stack(
            [jnp.where(swap, w_other, w_mine), jnp.where(swap, w_mine, w_other)], axis=0
        )
        w_all = w_all.transpose(2, 1, 0, 3, 4, 5)
        w_all = jnp.concatenate([w_all[:, :, :, 0], w_all[:, :, :, 1]], axis=-1)
        w_all = w_all.reshape(window, half)
        w = lambda i, j: w_all[i * width : (i + 1) * width, (j - 1) * width : j * width]
        f = lambda i, j: w(i, j).astype(F32)
        u = {(0, 1): -f(0, 1), (1, 2): -f(1, 2), (2, 3): -f(2, 3)}
        u[0, 2] = mm(w(0, 1), w(1, 2), None) - f(0, 2)
        u[1, 3] = mm(w(1, 2), w(2, 3), None) - f(1, 3)
        u[0, 3] = mm(w(0, 1), w(1, 3), None) - f(0, 3) - mm(u[0, 2], f(2, 3))
        columns = [
            jnp.concatenate([u[i, j] for i in range(j)], axis=0) for j in range(1, supernodes)
        ]

    def times_u(v):
        parts = [v[:, :width]]
        for j in range(1, supernodes):
            parts.append(v[:, j * width : (j + 1) * width] + mm(v[:, : j * width], columns[j - 1]))
        return jnp.concatenate(parts, axis=1)

    with jax.named_scope("cross"):
        right = times_u(product)
        left = times_u(panel_c.astype(F32))
        cross = lax.psum_scatter(
            right.reshape(ny, local, window), "y", scatter_dimension=0, tiled=True
        ).reshape(local, window)
        scale = jnp.repeat(select, width)[None, :]
        cross = -(scale * cross)

    with jax.named_scope("window"):
        tiles = []
        for t in range(supernodes):
            n = window - t * width
            part = mm_t(left[:, t * width : (t + 1) * width], right[:, t * width :])
            part = part.reshape(2, nx, nc, wlocal, n).transpose(2, 1, 3, 0, 4)
            tiles += [part[:, :, :, 0], part[:, :, :, 1]]
        packed = jnp.concatenate(tiles, axis=-1)
        packed = exchange(packed, "c").reshape(nc, nx, wlocal, -1).sum(0)
        packed = exchange(packed, "x").reshape(nx, wlocal, -1).sum(0)
        spread, at = [], 0
        for t in range(supernodes):
            n = window - t * width
            for _ in range(2):
                spread.append(jnp.pad(packed[:, at : at + n], ((0, 0), (window - n, 0))))
                at += n
        mine_w = exchange(jnp.stack(spread), "z").sum(0)
        mine_w = gather(mine_w, "y", ny).sum(0)

    with jax.named_scope("diagonal"):
        v_rows = []
        for k in range(supernodes):
            t_k = tile_inverse[k]
            blocks = [jnp.zeros((width, k * width), F32)] if k else []
            blocks.append(t_k)
            if k + 1 < supernodes:
                u_row = jnp.concatenate([u[k, j] for j in range(k + 1, supernodes)], axis=1)
                blocks.append(mm(t_k, u_row))
            v_rows.append(jnp.concatenate(blocks, axis=1))
        v_all = jnp.concatenate(v_rows, axis=0)
        v_mine = lax.dynamic_slice_in_dim(v_all, col * wlocal, wlocal, 1)
        base = mm_t(v_mine, v_all)
        keep = (jnp.arange(window, dtype=jnp.int32) // width) >= wtile
        block = jnp.where(keep[None, :], mine_w + base, 0.0)
    return cross, block


def solution(mesh):
    fine = Mesh(mesh.devices.reshape(8, 8, 4, 2), ("y", "z", "x", "c"))
    col = ("z", "x", "c")
    return jax.shard_map(
        body,
        mesh=fine,
        in_specs=(P("y", None, col, None), P(("y",) + col, None), P(col, None), P(), P()),
        out_specs=(P(("y",) + col, None), P(col, None)),
        check_vma=False,
    )
```

time: 1610 us -> 241 us (0.15)
  the two profiles are of different devices: /device:TPU:23 before, /device:TPU:2 now
where the time goes in v1:
time: 241 us; the launch traced here: 239 us
  blocking collectives  73.9 us (31%)
  local copies, waits for them, and re-layouts  59.6 us (25%)
  waiting for transfers between devices  32.4 us (13%)
  matrix products  21.7 us (9%)
  starting transfers between devices  18.3 us (8%)
  other arithmetic  18.3 us (8%)
  between operations  14.8 us (6%)
    all_to_all x3, blocking collectives, exchange(): return lax.all_to_all(x, axis, 0, 0, tiled=True)  73.9 us
    all_to_all x3, waiting for transfers between devices, exchange(): return lax.all_to_all(x, axis, 0, 0, tiled=True)  32.4 us
    all_to_all x3, starting transfers between devices, exchange(): return lax.all_to_all(x, axis, 0, 0, tiled=True)  16.3 us
    dynamic_slice x1, local copies, waits for them, and re-layouts, body(): other = lax.dynamic_index_in_dim(sigma, 1 - c, 2, keepdims=False)  13.8 us
    unnamed x56, local copies, waits for them, and re-layouts  11.9 us
    dot_general x17, matrix products, mm(): return jnp.dot(a, b, precision=precision, preferred_element_type=F32)  11 us
    dot_general x7, matrix products, mm_t(): lax.dot_general(a, b, (((0,), (0,)), ((), ())), precision=precision, pref...  10.7 us
    transpose x1, local copies, waits for them, and re-layouts, body(): mine = mine.transpose(1, 0, 2, 3).reshape(-1, ny * local)  10.3 us
  transfers between devices with their start and end apart: 6, of which 3 were waited for; matrix products, arithmetic and copies ran while one was open for 30% of the time, Pallas kernels for 0%

profile of v1, /device:TPU:2, one launch (start us, length us, event | category | flops | bytes accessed | tf_op | source)
XLA Modules:
  0.0 238.9 jit_solution(15479624505573740872)
XLA Ops:
  7.2 0.9 constant_dynamic-update-slice_fusion.1
  8.2 0.8 constant_dynamic-update-slice_fusion
  9.0 1.2 fusion.45
  10.2 1.2 fusion.42
  11.4 1.2 fusion.39
  12.6 0.9 fusion.105
  14.1 1.9 constant_dynamic-update-slice_fusion.14
  16.6 0.7 constant_dynamic-update-slice_fusion.12
  17.3 0.7 constant_dynamic-update-slice_fusion.11
  18.1 31.8 %all_to_all.30 = bf16[8,32,1408]{2,1,0:T(8,128)(2,1)S(1)} all-to-all(bf16[8,32,1408]{2,1,0:T(8,128)(2,1)S(1)} %broadcast_in_dim.43), channel_id=1, replica_groups=mesh['y'=8,'z'=8,'x'=4,'c'=2] {'z'}, dimensions={0} | all-to-all | bytes 1441792 | tf_op jit(solution)/shard_map/gather/all_to_all | solution.py:23
  50.2 36.1 %all_to_all.31 = bf16[4,256,1408]{2,1,0:T(8,128)(2,1)S(1)} all-to-all(bf16[4,256,1408]{2,1,0:T(8,128)(2,1)S(1)} %broadcast_in_dim.45), channel_id=1, replica_groups=mesh['y'=8,'z'=8,'x'=4,'c'=2] {'x'}, dimensions={0} | all-to-all | bytes 5767168 | tf_op jit(solution)/shard_map/gather/all_to_all | solution.py:23
  86.2 1.9 collective-permute-start
  88.2 9.9 %reshape.118 = bf16[8,4,2,32,256]{3,2,1,0,4:T(2,128)(2,1)} reshape(bf16[2048,8,1,32]{0,3,2,1:T(8,128)(2,1)} %param.5) | data formatting | bytes 2097152 | tf_op jit(solution)/shard_map/sigma/reshape | solution.py:67
  98.1 13.8 %constant_dynamic-slice_fusion = (bf16[8,4,1,32,256]{3,2,1,0,4:T(2,128)(2,1)}, bf16[8,4,1,32,256]{3,2,1,0,4:T(2,128)(2,1)}) fusion(bf16[8,4,2,32,256]{3,2,1,0,4:T(2,128)(2,1)} %reshape.118, s32[]{:T(128)S(6)} %select_n.70, s32[]{:T(128)S(6)} %select_n.68), kind=kLoop, calls=%fused_computation.159 | loop fusion | bytes 2097160 | tf_op jit(solution)/shard_map/sigma/jit(dynamic_index_in_dim)/dynamic_slice | solution.py:69
  111.8 10.3 %copy.68 = bf16[8,4,1,32,256]{4,3,0,1,2:T(8,128)(2,1)} copy(bf16[8,4,1,32,256]{3,2,1,0,4:T(2,128)(2,1)} %get-tuple-element.15) | data formatting | bytes 1048576 | tf_op jit(solution)/shard_map/sigma/transpose | solution.py:70
  122.1 8.9 %copy.69 = bf16[8,4,1,32,256]{4,3,0,1,2:T(8,128)(2,1)S(1)} copy(bf16[8,4,1,32,256]{3,2,1,0,4:T(2,128)(2,1)} %get-tuple-element.14) | data formatting | bytes 1048576 | tf_op jit(solution)/shard_map/sigma/transpose | solution.py:71
  131.0 1.1 slice_convert_fusion
  132.2 1.8 fusion.2
  134.0 1.3 broadcast_select_fusion.1
  135.9 0.8 convert_negate_fusion.1
  137.3 2.4 %fusion.4 = f32[256,1024]{1,0:T(8,128)S(1)} fusion(f32[256,1024]{1,0:T(8,128)S(1)} %fusion.2, bf16[1024,256]{1,0:T(8,128)(2,1)S(1)} %bitcast.171, bf16[1024,1408]{1,0:T(8,128)(2,1)} %collective-permute-done), kind=kOutput, calls=%fused_computation.7 | convolution fusion | flops 537133056 | bytes 4718592 | tf_op jit(solution)/shard_map/gather/dot_general | solution.py:17
  144.7 6.0 %all_to_all.32 = f32[2,4,16,5120]{3,2,1,0:T(8,128)S(1)} all-to-all(f32[2,4,16,5120]{3,2,1,0:T(8,128)S(1)} %fusion.49), channel_id=1, replica_groups=mesh['y'=8,'z'=8,'x'=4,'c'=2] {'c'}, dimensions={0} | all-to-all | bytes 5242880 | tf_op jit(solution)/shard_map/window/all_to_all | solution.py:23
  150.7 1.4 reduce_sum.36
  152.1 5.0 %all-to-all-start.3 = ((f32[4,16,5120]{2,1,0:T(8,128)}), f32[4,16,5120]{2,1,0:T(8,128)S(1)}, u32[]{:S(2)}, u32[]{:S(2)}) async-start(f32[4,16,5120]{2,1,0:T(8,128)} %reduce_sum.36), calls=%async_computation.4 | async-start | bytes 2621440 | tf_op jit(solution)/shard_map/window/all_to_all | solution.py:23
  157.1 2.3 pad_maximum_fusion
  159.4 14.7 %all-to-all-done.3 = f32[4,16,5120]{2,1,0:T(8,128)S(1)} async-done(((f32[4,16,5120]{2,1,0:T(8,128)}), f32[4,16,5120]{2,1,0:T(8,128)S(1)}, u32[]{:S(2)}, u32[]{:S(2)}) %all-to-all-start.3) | async-done | bytes 1310752 | tf_op jit(solution)/shard_map/window/all_to_all | solution.py:23
  174.2 0.6 fusion.64
  174.8 0.6 fusion.63
  176.1 0.6 constant_dynamic-update-slice_fusion.19
  177.4 0.6 constant_dynamic-update-slice_fusion.17
  178.0 0.6 constant_dynamic-update-slice_fusion.16
  178.6 0.6 constant_dynamic-update-slice_fusion.15
  179.3 4.1 %all-to-all-start.4 = ((f32[8,16,1024]{2,1,0:T(8,128)}), f32[8,16,1024]{2,1,0:T(8,128)}, u32[]{:S(2)}, u32[]{:S(2)}) async-start(f32[8,16,1024]{2,1,0:T(8,128)} %constant_dynamic-update-slice_fusion.15), calls=%async_computation.5 | async-start | bytes 1048576 | tf_op jit(solution)/shard_map/window/all_to_all | solution.py:23
  183.5 0.9 fusion.107
  184.4 1.8 copy.66
  186.2 1.8 copy.65
  188.0 1.8 copy.64
  189.8 0.8 copy.63
  190.7 1.4 convolution_bitcast_fusion.1
  192.1 0.8 convolution_bitcast_fusion
  192.9 7.7 %all-to-all-done.4 = f32[8,16,1024]{2,1,0:T(8,128)} async-done(((f32[8,16,1024]{2,1,0:T(8,128)}), f32[8,16,1024]{2,1,0:T(8,128)}, u32[]{:S(2)}, u32[]{:S(2)}) %all-to-all-start.4) | async-done | bytes 524320 | tf_op jit(solution)/shard_map/window/all_to_all | solution.py:23
  200.7 1.1 reduce_sum.38
  201.7 0.9 broadcast_in_dim.47
  202.6 7.2 %all-to-all-start.5 = ((f32[8,16,1024]{2,1,0:T(8,128)}), f32[8,16,1024]{2,1,0:T(8,128)S(1)}, u32[]{:S(2)}, u32[]{:S(2)}) async-start(f32[8,16,1024]{2,1,0:T(8,128)} %broadcast_in_dim.47), calls=%async_computation.6 | async-start | bytes 1048576 | tf_op jit(solution)/shard_map/window/all_to_all | solution.py:23
  210.2 5.6 %select_maximum_fusion = f32[1024,1024]{0,1:T(8,128)} fusion(f32[256,256]{0,1:T(8,128)} %bitcast.179, f32[256,256]{0,1:T(8,128)S(1)} %convolution_bitcast_fusion.2, f32[256,256]{0,1:T(8,128)} %bitcast.180, f32[256,512]{0,1:T(8,128)S(1)} %broadcast_in_dim.49, f32[256,512]{0,1:T(8,128)} %convolution_bitcast_fusion.1, f32[256,256]{0,1:T(8,128)} %bitcast.181, ...), kind=kLoop, calls=%fused_computation | loop fusion | flops 10485760 | bytes 7602176 | tf_op jit(solution)/shard_map/diagonal/concatenate | solution.py:144
  215.9 1.6 fusion.51
  217.4 10.0 %all-to-all-done.5 = f32[8,16,1024]{2,1,0:T(8,128)S(1)} async-done(((f32[8,16,1024]{2,1,0:T(8,128)}), f32[8,16,1024]{2,1,0:T(8,128)S(1)}, u32[]{:S(2)}, u32[]{:S(2)}) %all-to-all-start.5) | async-done | bytes 524320 | tf_op jit(solution)/shard_map/window/all_to_all | solution.py:23
  227.4 4.7 %fusion.7 = f32[16,1024]{1,0:T(8,128)} fusion(f32[16,1024]{1,0:T(8,128)S(1)} %reduce_sum.39, f32[1024,1024]{0,1:T(8,128)} %select_maximum_fusion, s32[]{:T(128)S(6)} %select_n.77, pred[1024]{0:T(1024)(128)(4,1)S(1)} %fusion.77), kind=kOutput, calls=%fused_computation.19 | convolution fusion | flops 100696064 | bytes 4391940 | tf_op jit(solution)/shard_map/diagonal/dot_general | solution.py:17
  (94 shorter events, 9.4 us)
Async XLA Ops:
  7.2 123.9 %all-gather.2.cloned.1.call-start = ((), (), s32[]{:S(2)}) async-start(), calls=%async_computation.8 | async-start | bytes 1179648 | tf_op jit(solution)/shard_map/column_block/all_gather | solution.py:64
  18.0 32.1 %copy-start.15 = (bf16[32,2048]{1,0:T(8,128)(2,1)}, bf16[32,2048]{1,0:T(8,128)(2,1)S(1)}, u32[]{:S(2)}) copy-start(bf16[32,2048]{1,0:T(8,128)(2,1)S(1)} %get-tuple-element.30) | copy-start | bytes 393220
  86.2 47.7 %collective-permute-start = (bf16[1024,1408]{1,0:T(8,128)(2,1)S(1)}, bf16[1024,1408]{1,0:T(8,128)(2,1)}, u32[]{:S(2)}, u32[]{:S(2)}) collective-permute-start(bf16[1024,1408]{1,0:T(8,128)(2,1)S(1)} %bitcast.153), channel_id=1, source_target_pairs={{0,1},{1,0},{2,3},{3,2},{4,5},{5,4},{6,7},{7,6},{8,9},{9,8},{10,11... | collective-permute-start | bytes 8650760 | tf_op jit(solution)/shard_map/gather/ppermute | solution.py:76
  136.7 6.2 %copy-start.5 = (f32[256,256]{1,0:T(8,128)}, f32[256,256]{1,0:T(8,128)S(1)}, u32[]{:S(2)}) copy-start(f32[256,256]{1,0:T(8,128)S(1)} %get-tuple-element.10) | copy-start | bytes 786436
  137.1 6.7 %copy-start.10 = (f32[256,256]{1,0:T(8,128)}, f32[256,256]{1,0:T(8,128)S(1)}, u32[]{:S(2)}) copy-start(f32[256,256]{1,0:T(8,128)S(1)} %convolution_subtract_fusion) | copy-start | bytes 786436
  137.3 5.7 %copy-start.2 = (f32[256,256]{1,0:T(8,128)}, f32[256,256]{1,0:T(8,128)S(1)}, u32[]{:S(2)}) copy-start(f32[256,256]{1,0:T(8,128)S(1)} %convolution_subtract_fusion.3) | copy-start | bytes 786436
  139.7 1.5 copy-start.13
  140.0 2.2 copy-start.7
  140.0 1.7 copy-start.12
  140.3 3.5 %copy-start.8 = (f32[256,256]{1,0:T(8,128)}, f32[256,256]{1,0:T(8,128)S(1)}, u32[]{:S(2)}) copy-start(f32[256,256]{1,0:T(8,128)S(1)} %convolution_subtract_fusion.1) | copy-start | bytes 786436
  140.7 2.5 %copy-start.4 = (f32[256,256]{1,0:T(8,128)}, f32[256,256]{1,0:T(8,128)S(1)}, u32[]{:S(2)}) copy-start(f32[256,256]{1,0:T(8,128)S(1)} %slice_add_fusion.1) | copy-start | bytes 786436
  141.3 3.0 %copy-start = (f32[256,256]{1,0:T(8,128)}, f32[256,256]{1,0:T(8,128)S(1)}, u32[]{:S(2)}) copy-start(f32[256,256]{1,0:T(8,128)S(1)} %slice_add_fusion) | copy-start | bytes 786436
  152.1 22.0 %all-to-all-start.3 = ((f32[4,16,5120]{2,1,0:T(8,128)}), f32[4,16,5120]{2,1,0:T(8,128)S(1)}, u32[]{:S(2)}, u32[]{:S(2)}) async-start(f32[4,16,5120]{2,1,0:T(8,128)} %reduce_sum.36), calls=%async_computation.4 | async-start | bytes 2621440 | tf_op jit(solution)/shard_map/window/all_to_all | solution.py:23
  157.1 58.8 %reduce-scatter.2.cloned.1.call-start = ((), (), s32[]{:S(2)}) async-start(), calls=%async_computation.7 | async-start | bytes 1179648 | tf_op jit(solution)/shard_map/cross/reduce_scatter | solution.py:109
  159.4 24.1 %copy-start.1 = (f32[4,256,256]{2,1,0:T(8,128)S(1)}, f32[4,256,256]{2,1,0:T(8,128)}, u32[]{:S(2)}) copy-start(f32[4,256,256]{2,1,0:T(8,128)} %param.8) | copy-start | bytes 3145732
  176.1 14.6 %copy-start.6 = (f32[256,256]{1,0:T(8,128)S(1)}, f32[256,256]{1,0:T(8,128)}, u32[]{:S(2)}) copy-start(f32[256,256]{1,0:T(8,128)} %copy-done.5) | copy-start | bytes 786436
  176.1 14.6 %copy-start.11 = (f32[256,256]{1,0:T(8,128)S(1)}, f32[256,256]{1,0:T(8,128)}, u32[]{:S(2)}) copy-start(f32[256,256]{1,0:T(8,128)} %copy-done.10) | copy-start | bytes 786436
  179.3 21.4 %all-to-all-start.4 = ((f32[8,16,1024]{2,1,0:T(8,128)}), f32[8,16,1024]{2,1,0:T(8,128)}, u32[]{:S(2)}, u32[]{:S(2)}) async-start(f32[8,16,1024]{2,1,0:T(8,128)} %constant_dynamic-update-slice_fusion.15), calls=%async_computation.5 | async-start | bytes 1048576 | tf_op jit(solution)/shard_map/window/all_to_all | solution.py:23
  183.4 8.7 %copy-start.3 = (f32[256,256]{1,0:T(8,128)S(1)}, f32[256,256]{1,0:T(8,128)}, u32[]{:S(2)}) copy-start(f32[256,256]{1,0:T(8,128)} %copy-done.2) | copy-start | bytes 786436
  183.4 8.7 %copy-start.9 = (f32[256,256]{1,0:T(8,128)S(1)}, f32[256,256]{1,0:T(8,128)}, u32[]{:S(2)}) copy-start(f32[256,256]{1,0:T(8,128)} %copy-done.8) | copy-start | bytes 786436
  183.4 8.7 %copy-start.14 = (f32[256,256]{1,0:T(8,128)S(1)}, f32[256,256]{1,0:T(8,128)}, u32[]{:S(2)}) copy-start(f32[256,256]{1,0:T(8,128)} %get-tuple-element.22) | copy-start | bytes 786436
  202.6 24.8 %all-to-all-start.5 = ((f32[8,16,1024]{2,1,0:T(8,128)}), f32[8,16,1024]{2,1,0:T(8,128)S(1)}, u32[]{:S(2)}, u32[]{:S(2)}) async-start(f32[8,16,1024]{2,1,0:T(8,128)} %broadcast_in_dim.47), calls=%async_computation.6 | async-start | bytes 1048576 | tf_op jit(solution)/shard_map/window/all_to_all | solution.py:23
Sparse Core Ops, SparseCore 0:
  88.3 37.6 all-gather.1
  160.7 38.5 reduce-scatter.1

commit v2 on v1

v2 whole, which is shorter than its diff:
```python
import jax
import jax.numpy as jnp
from jax import lax
from jax.experimental import pallas as pl
from jax.experimental.pallas import tpu as pltpu
from jax.sharding import Mesh, PartitionSpec as P

HIGHEST = lax.Precision.HIGHEST
HIGH = lax.Precision.HIGH
BF16 = jnp.bfloat16
F32 = jnp.float32


def mm(a, b, precision=HIGH):
    return jnp.dot(a, b, precision=precision, preferred_element_type=F32)


def mm_t(a, b, precision=HIGH):
    return lax.dot_general(
        a, b, (((0,), (0,)), ((), ())), precision=precision, preferred_element_type=F32
    )


def exchange(x, axis):
    return lax.all_to_all(x, axis, 0, 0, tiled=True)


def gather(x, axis, size):
    return exchange(jnp.broadcast_to(x[None], (size,) + x.shape), axis)


def local_call(kernel, shapes, scalars, *arrays):
    vmem = pl.BlockSpec(memory_space=pltpu.VMEM)
    smem = pl.BlockSpec(memory_space=pltpu.SMEM)
    return pl.pallas_call(
        kernel,
        out_shape=shapes,
        in_specs=[smem] * len(scalars) + [vmem] * len(arrays),
        out_specs=jax.tree.map(lambda _: vmem, shapes),
        compiler_params=pltpu.CompilerParams(vmem_limit_bytes=40 * 1024 * 1024),
    )(*scalars, *arrays)


def panel_kernel(scale_ref, a_ref, w_ref, t_ref, message_ref, panel_ref):
    supernodes, width = t_ref.shape[0], t_ref.shape[1]
    local, wlocal = a_ref.shape[0], w_ref.shape[0]
    ha = supernodes * width // 2
    hw = (supernodes - 1) * width // 2
    for h in range(2):
        message_ref[h, local:, hw:] = jnp.zeros((wlocal, ha - hw), BF16)
    for j in range(supernodes):
        at = slice(j * width, (j + 1) * width)
        rows = jnp.concatenate([a_ref[:, at], w_ref[:, at]], axis=0)
        product = mm(rows, t_ref[j], HIGHEST)
        a = (scale_ref[j] * product[:local]).astype(BF16)
        panel_ref[:, at] = a
        h, off = divmod(j * width, ha)
        message_ref[h, :local, off : off + width] = a
        if j == 0:
            continue
        w = (scale_ref[supernodes + j] * product[local:]).astype(BF16)
        for piece in range(2):
            start = (j - 1) * width + piece * (width // 2)
            h, off = divmod(start, hw)
            message_ref[h, local:, off : off + width // 2] = w[
                :, piece * (width // 2) : (piece + 1) * (width // 2)
            ]


def sum_kernel(in_ref, out_ref):
    total = in_ref[0]
    for i in range(1, in_ref.shape[0]):
        total = total + in_ref[i]
    out_ref[...] = total


def spread_kernel(in_ref, out_ref):
    width = out_ref.shape[2] // 4
    at = 0
    for i in range(out_ref.shape[0]):
        edge = (i // 2) * width
        n = out_ref.shape[2] - edge
        total = in_ref[0, :, at : at + n]
        for k in range(1, in_ref.shape[0]):
            total = total + in_ref[k, :, at : at + n]
        if edge:
            out_ref[i, :, :edge] = jnp.zeros((out_ref.shape[1], edge), F32)
        out_ref[i, :, edge:] = total
        at += n


def repeat_kernel(in_ref, out_ref):
    total = in_ref[0]
    for i in range(1, in_ref.shape[0]):
        total = total + in_ref[i]
    for i in range(out_ref.shape[0]):
        out_ref[i] = total


def finish_kernel(tile_ref, in_ref, base_ref, out_ref):
    total = base_ref[...]
    for i in range(in_ref.shape[0]):
        total = total + in_ref[i]
    columns = lax.broadcasted_iota(jnp.int32, total.shape, 1)
    out_ref[...] = jnp.where(columns >= tile_ref[0] * (total.shape[1] // 4), total, 0.0)


def body(sigma_top, ancestor_rows, window_rows, tile_inverse, structure):
    ny, nz, nx, nc = 8, 8, 4, 2
    supernodes, width = tile_inverse.shape[0], tile_inverse.shape[1]
    window = supernodes * width
    local = ancestor_rows.shape[0]
    wlocal = window_rows.shape[0]
    y, z, x, c = (lax.axis_index(name) for name in ("y", "z", "x", "c"))
    col = (z * nx + x) * nc + c
    tile = ((y * (nz * nx * nc) + col) * local) // width
    wtile = (col * wlocal) // width
    select = lax.dynamic_slice_in_dim(structure, tile, 1, 1)[:, 0].astype(F32)

    with jax.named_scope("panels"):
        ha, hw = window // 2, (window - width) // 2
        keep = (wtile < jnp.arange(supernodes, dtype=jnp.int32)).astype(F32)
        message, panel = local_call(
            panel_kernel,
            (
                jax.ShapeDtypeStruct((nc, local + wlocal, ha), BF16),
                jax.ShapeDtypeStruct((local, window), BF16),
            ),
            (jnp.concatenate([select, keep]),),
            ancestor_rows,
            window_rows,
            tile_inverse,
        )

    with jax.named_scope("gather"):
        got = exchange(message, "c").reshape(nc, local + wlocal, ha)
        got = lax.all_gather(got, "x", axis=0, tiled=True)
        half = lax.all_gather(got[:, :local].reshape(-1, ha), "z", axis=0, tiled=True)
        wgot = got[:, local:, :hw].reshape(-1, hw)
        whalf = gather(wgot, "z", nz).reshape(window, hw)[: window - width]
        swap = [(0, 1), (1, 0)]
        sibling = lax.ppermute(half, "c", swap)
        wsibling = lax.ppermute(whalf, "c", swap)
        first = c == 0

    with jax.named_scope("column_block"):
        panel_c = gather(panel, "y", ny).reshape(ny * local, window)

    with jax.named_scope("sigma"):
        sigma = sigma_top.transpose(1, 2, 3, 0).reshape(ny * local, -1)
        own = mm(sigma, half, None)
        away = mm(sigma, sibling, None)
        product = jnp.concatenate(
            [jnp.where(first, own, away), jnp.where(first, away, own)], axis=1
        )

    with jax.named_scope("unit_inverse"):
        w_all = jnp.concatenate(
            [jnp.where(first, whalf, wsibling), jnp.where(first, wsibling, whalf)], axis=1
        )
        w = lambda i, j: w_all[i * width : (i + 1) * width, (j - 1) * width : j * width]
        f = lambda i, j: w(i, j).astype(F32)
        u = {(0, 1): -f(0, 1), (1, 2): -f(1, 2), (2, 3): -f(2, 3)}
        u[0, 2] = mm(w(0, 1), w(1, 2), None) - f(0, 2)
        u[1, 3] = mm(w(1, 2), w(2, 3), None) - f(1, 3)
        u[0, 3] = mm(w(0, 1), w(1, 3), None) - f(0, 3) - mm(u[0, 2], f(2, 3))
        columns = [
            jnp.concatenate([u[i, j] for i in range(j)], axis=0) for j in range(1, supernodes)
        ]

    def times_u(v):
        parts = [v[:, :width]]
        for j in range(1, supernodes):
            parts.append(v[:, j * width : (j + 1) * width] + mm(v[:, : j * width], columns[j - 1]))
        return jnp.concatenate(parts, axis=1)

    with jax.named_scope("cross"):
        right = times_u(product)
        left = times_u(panel_c.astype(F32))
        cross = lax.psum_scatter(
            right.reshape(ny, local, window), "y", scatter_dimension=0, tiled=True
        ).reshape(local, window)
        scale = jnp.repeat(select, width)[None, :]
        cross = -(scale * cross)

    with jax.named_scope("window"):
        tiles = []
        for t in range(supernodes):
            n = window - t * width
            part = mm_t(left[:, t * width : (t + 1) * width], right[:, t * width :])
            part = part.reshape(2, nx, nc, wlocal, n).transpose(2, 1, 3, 0, 4)
            tiles += [part[:, :, :, 0], part[:, :, :, 1]]
        packed = jnp.concatenate(tiles, axis=-1)
        shape = lambda *dims: jax.ShapeDtypeStruct(dims, F32)
        n = packed.shape[-1]
        packed = exchange(packed, "c")
        packed = local_call(sum_kernel, shape(nx, wlocal, n), (), packed)
        packed = exchange(packed, "x")
        spread = local_call(spread_kernel, shape(nz, wlocal, window), (), packed)
        spread = exchange(spread, "z")
        spread = local_call(repeat_kernel, shape(ny, wlocal, window), (), spread)
        spread = exchange(spread, "y")

    with jax.named_scope("diagonal"):
        v_rows = []
        for k in range(supernodes):
            t_k = tile_inverse[k]
            blocks = [jnp.zeros((width, k * width), F32)] if k else []
            blocks.append(t_k)
            if k + 1 < supernodes:
                u_row = jnp.concatenate([u[k, j] for j in range(k + 1, supernodes)], axis=1)
                blocks.append(mm(t_k, u_row))
            v_rows.append(jnp.concatenate(blocks, axis=1))
        v_all = jnp.concatenate(v_rows, axis=0)
        v_mine = lax.dynamic_slice_in_dim(v_all, col * wlocal, wlocal, 1)
        base = mm_t(v_mine, v_all)
        block = local_call(
            finish_kernel, shape(wlocal, window), (wtile.reshape(1),), spread, base
        )
    return cross, block


def solution(mesh):
    fine = Mesh(mesh.devices.reshape(8, 8, 4, 2), ("y", "z", "x", "c"))
    col = ("z", "x", "c")
    return jax.shard_map(
        body,
        mesh=fine,
        in_specs=(P("y", None, col, None), P(("y",) + col, None), P(col, None), P(), P()),
        out_specs=(P(("y",) + col, None), P(col, None)),
        check_vma=False,
    )
```

time: 241 us -> 180 us (0.75)
  local copies, waits for them, and re-layouts: 59.6 us -> 18.2 us
  blocking collectives: 73.9 us -> 57.7 us
  other arithmetic: 18.3 us -> 11.9 us
  matrix products: 21.7 us -> 15.4 us
  starting transfers between devices: 18.3 us -> 22.9 us
  Pallas kernels: 0 us -> 2.94 us
  waiting for transfers between devices: 32.4 us -> 35.1 us
    all_to_all x3, blocking collectives: 73.9 us -> 42.3 us  [exchange(): return lax.all_to_all(x, axis, 0, 0, tiled=True)]
    transpose x2 -> x0, local copies, waits for them, and re-layouts: 19.2 us -> none  [the longest x1 10.3 us: body(): mine = mine.transpose(1, 0, 2, 3).reshape(-1, ny * local)]
    all_gather x0 -> x1, blocking collectives: none -> 15.3 us  [body(): got = lax.all_gather(got, 'x', axis=0, tiled=True)]
    dynamic_slice x1 -> x0, local copies, waits for them, and re-layouts: 13.8 us -> none  [body(): other = lax.dynamic_index_in_dim(sigma, 1 - c, 2, keepdims=False)]
    reshape x1 -> x0, local copies, waits for them, and re-layouts: 9.91 us -> none  [body(): sigma = sigma_top.reshape(nz, nx, nc, local, ny * local)]
    dot_general x7 -> x5, matrix products: 10.7 us -> 4.21 us  [mm_t(): lax.dot_general(a, b, (((0,), (0,)), ((), ())), precision=precision, pref...]
    pallas_call x0 -> x5, Pallas kernels: none -> 2.94 us  [local_call(): pl.pallas_call(kernel, out_shape=shapes, in_specs=[smem] * len(scalars) +...]
    all_to_all x3 -> x4, starting transfers between devices: 16.3 us -> 19 us  [exchange(): return lax.all_to_all(x, axis, 0, 0, tiled=True)]
  transfers between devices with their start and end apart: 6 -> 8, of which waited for: 3 -> 5; matrix products, arithmetic and copies ran while one was open for 30% -> 19% of each run, Pallas kernels for 0% -> 1%
where the time goes in v2:
time: 180 us; the launch traced here: 179 us
  blocking collectives  57.7 us (32%)
  waiting for transfers between devices  35.1 us (20%)
  starting transfers between devices  22.9 us (13%)
  local copies, waits for them, and re-layouts  18.2 us (10%)
  matrix products  15.4 us (9%)
  between operations  14.7 us (8%)
  other arithmetic  11.9 us (7%)
  Pallas kernels  2.94 us (2%)
    all_to_all x3, blocking collectives, exchange(): return lax.all_to_all(x, axis, 0, 0, tiled=True)  42.3 us
    all_to_all x4, waiting for transfers between devices, exchange(): return lax.all_to_all(x, axis, 0, 0, tiled=True)  34.4 us
    all_to_all x4, starting transfers between devices, exchange(): return lax.all_to_all(x, axis, 0, 0, tiled=True)  19 us
    all_gather x1, blocking collectives, body(): got = lax.all_gather(got, 'x', axis=0, tiled=True)  15.3 us
    unnamed x59, local copies, waits for them, and re-layouts  12.7 us
    dot_general x15, matrix products, mm(): return jnp.dot(a, b, precision=precision, preferred_element_type=F32)  11.2 us
    dot_general x5, matrix products, mm_t(): lax.dot_general(a, b, (((0,), (0,)), ((), ())), precision=precision, pref...  4.21 us
    concatenate x1, other arithmetic, body(): v_all = jnp.concatenate(v_rows, axis=0)  3.82 us
  transfers between devices with their start and end apart: 8, of which 5 were waited for; matrix products, arithmetic and copies ran while one was open for 19% of the time, Pallas kernels for 1%

profile of v2, /device:TPU:2, one launch (start us, length us, event | category | flops | bytes accessed | tf_op | source)
XLA Modules:
  0.0 178.7 jit_solution(7130280223805997884)
XLA Ops:
  7.3 0.9 convert_reduce_fusion
  8.3 1.2 copy-done.1
  9.5 0.9 copy-done.5
  10.4 0.8 copy-done.6
  11.3 1.2 panels.1
  12.5 3.8 %all_to_all.35 = bf16[2,48,512]{2,1,0:T(8,128)(2,1)S(1)} all-to-all(bf16[2,48,512]{2,1,0:T(8,128)(2,1)S(1)} %get-tuple-element.4), channel_id=1, replica_groups=mesh['y'=8,'z'=8,'x'=4,'c'=2] {'c'}, dimensions={0} | all-to-all | bytes 196608 | tf_op jit(solution)/shard_map/gather/all_to_all | solution.py:25
  16.3 15.3 %all_gather.6 = bf16[8,48,512]{2,1,0:T(8,128)(2,1)S(1)} all-gather(bf16[2,48,512]{2,1,0:T(8,128)(2,1)S(1)} %all_to_all.35), channel_id=1, replica_groups=mesh['y'=8,'z'=8,'x'=4,'c'=2] {'x'}, dimensions={0}, use_global_device_ids=true | all-gather | bytes 491520 | tf_op jit(solution)/shard_map/gather/all_gather | solution.py:137
  31.6 0.7 slice.145
  32.5 32.7 %all_to_all.36 = bf16[8,128,384]{2,1,0:T(8,128)(2,1)S(1)} all-to-all(bf16[8,128,384]{2,1,0:T(8,128)(2,1)S(1)} %broadcast_in_dim.25), channel_id=1, replica_groups=mesh['y'=8,'z'=8,'x'=4,'c'=2] {'z'}, dimensions={0} | all-to-all | bytes 1572864 | tf_op jit(solution)/shard_map/gather/all_to_all | solution.py:25
  65.2 0.9 broadcast_in_dim.26
  66.0 7.2 %all-to-all-start.2 = ((bf16[8,32,1024]{2,1,0:T(8,128)(2,1)}), bf16[8,32,1024]{2,1,0:T(8,128)(2,1)S(1)}, u32[]{:S(2)}, u32[]{:S(2)}) async-start(bf16[8,32,1024]{2,1,0:T(8,128)(2,1)} %broadcast_in_dim.26), calls=%async_computation.3 | async-start | bytes 1048576 | tf_op jit(solution)/shard_map/column_block/all_to_all | solution.py:25
  73.3 1.9 %collective-permute-start.1 = (bf16[768,384]{1,0:T(8,128)(2,1)S(1)}, bf16[768,384]{1,0:T(8,128)(2,1)}, u32[]{:S(2)}, u32[]{:S(2)}) collective-permute-start(bf16[768,384]{1,0:T(8,128)(2,1)S(1)} %bitcast.115), channel_id=1, source_target_pairs={{0,1},{1,0},{2,3},{3,2},{4,5},{5,4},{6,7},{7,6},{8,9},{9,8},{10,11... | collective-permute-start | bytes 1769480 | tf_op jit(solution)/shard_map/gather/ppermute | solution.py:143
  75.3 11.3 %all-to-all-done.2 = bf16[8,32,1024]{2,1,0:T(8,128)(2,1)S(1)} async-done(((bf16[8,32,1024]{2,1,0:T(8,128)(2,1)}), bf16[8,32,1024]{2,1,0:T(8,128)(2,1)S(1)}, u32[]{:S(2)}, u32[]{:S(2)}) %all-to-all-start.2) | async-done | bytes 524320 | tf_op jit(solution)/shard_map/column_block/all_to_all | solution.py:25
  86.6 1.1 bitcast_convert_fusion
  87.7 1.2 broadcast_select_fusion.1
  88.9 1.9 %collective-permute-start = (bf16[2048,512]{1,0:T(8,128)(2,1)}, bf16[2048,512]{1,0:T(8,128)(2,1)S(1)}, u32[]{:S(2)}, u32[]{:S(2)}) collective-permute-start(bf16[2048,512]{1,0:T(8,128)(2,1)} %all-gather.2.cloned.1.call-done), channel_id=1, source_target_pairs={{0,1},{1,0},{2,3},{3,2},{4,5},{5,4},{6,7},{7,6},{8,9},{9,8},{10,11... | collective-permute-start | bytes 6291464 | tf_op jit(solution)/shard_map/gather/ppermute | solution.py:142
  90.9 0.8 convert_negate_fusion.1
  93.8 0.8 fusion.64
  94.6 0.6 collective-permute-done
  95.2 0.8 fusion.65
  96.1 0.6 slice_add_fusion.1
  96.7 0.8 slice_add_fusion
  98.4 0.6 fusion.16
  99.1 0.8 fusion.3
  100.9 5.8 %all_to_all.37.in_ref = f32[2,4,16,5120]{3,2,1,0:T(8,128)S(1)} all-to-all(f32[2,4,16,5120]{3,2,1,0:T(8,128)S(1)} %fusion.34), channel_id=1, replica_groups=mesh['y'=8,'z'=8,'x'=4,'c'=2] {'c'}, dimensions={0} | all-to-all | bytes 5242880 | tf_op jit(solution)/shard_map/window/all_to_all | solution.py:25
  106.9 1.0 copy-done.3
  107.9 4.5 %all-to-all-start.4 = ((f32[4,16,5120]{2,1,0:T(8,128)}), f32[4,16,5120]{2,1,0:T(8,128)S(1)}, u32[]{:S(2)}, u32[]{:S(2)}) async-start(f32[4,16,5120]{2,1,0:T(8,128)} %copy-done.3), calls=%async_computation.5 | async-start | bytes 2621440 | tf_op jit(solution)/shard_map/window/all_to_all | solution.py:25
  112.4 2.3 %pad_maximum_fusion = f32[256,1024]{0,1:T(8,128)} fusion(f32[256,256]{0,1:T(8,128)} %copy-done.8, f32[256,256]{0,1:T(8,128)} %copy-done.11, f32[256,256]{0,1:T(8,128)} %copy-done.13, f32[256,256]{0,1:T(8,128)} %copy-done.19), kind=kLoop, calls=%fused_computation.13 | loop fusion | flops 786432 | bytes 2097152 | tf_op jit(solution)/shard_map/cross/concatenate | solution.py:175
  114.8 2.5 %copy.21 = f32[256,1024]{1,0:T(8,128)} copy(f32[256,1024]{0,1:T(8,128)} %pad_maximum_fusion) | data formatting | bytes 2097152 | tf_op jit(solution)/shard_map/cross/concatenate | solution.py:175
  117.3 1.0 fusion.63
  118.4 1.8 copy.30
  120.1 1.8 %copy.31 = f32[1,256,256]{1,2,0:T(8,128)} copy(f32[1,256,256]{2,1,0:T(8,128)} %get-tuple-element.12) | data formatting | bytes 524288
  121.9 1.8 %copy.32 = f32[1,256,256]{1,2,0:T(8,128)} copy(f32[1,256,256]{2,1,0:T(8,128)} %get-tuple-element.11) | data formatting | bytes 524288
  123.7 1.8 %copy.33 = f32[1,256,256]{1,2,0:T(8,128)} copy(f32[1,256,256]{2,1,0:T(8,128)} %get-tuple-element.13) | data formatting | bytes 524288
  125.5 3.6 %all-to-all-done.4.in_ref = f32[4,16,5120]{2,1,0:T(8,128)S(1)} async-done(((f32[4,16,5120]{2,1,0:T(8,128)}), f32[4,16,5120]{2,1,0:T(8,128)S(1)}, u32[]{:S(2)}, u32[]{:S(2)}) %all-to-all-start.4) | async-done | bytes 1310752 | tf_op jit(solution)/shard_map/window/all_to_all | solution.py:25
  129.2 0.8 copy-done.4
  130.0 3.8 %all-to-all-start.5 = ((f32[8,16,1024]{2,1,0:T(8,128)}), f32[8,16,1024]{2,1,0:T(8,128)S(1)}, u32[]{:S(2)}, u32[]{:S(2)}) async-start(f32[8,16,1024]{2,1,0:T(8,128)} %copy-done.4), calls=%async_computation.6 | async-start | bytes 1048576 | tf_op jit(solution)/shard_map/window/all_to_all | solution.py:25
  133.9 2.0 %convolution_bitcast_fusion.2 = f32[256,256]{0,1:T(8,128)} fusion(bf16[768,384]{1,0:T(8,128)(2,1)} %copy-done.7, f32[4,256,256]{2,1,0:T(8,128)S(1)} %copy-done.2), kind=kOutput, calls=%fused_computation.4 | convolution fusion | flops 100794368 | bytes 655360 | tf_op jit(solution)/shard_map/diagonal/dot_general | solution.py:15
  135.9 2.4 %convolution_bitcast_fusion.1 = f32[256,512]{0,1:T(8,128)} fusion(f32[256,256]{1,0:T(8,128)} %copy-done.17, f32[256,256]{1,0:T(8,128)} %copy-done.12, f32[4,256,256]{2,1,0:T(8,128)S(1)} %copy-done.2), kind=kOutput, calls=%fused_computation.3 | convolution fusion | flops 201457664 | bytes 1310720 | tf_op jit(solution)/shard_map/diagonal/dot_general | solution.py:15
  138.4 1.7 convolution_bitcast_fusion
  140.1 10.4 %all-to-all-done.5.in_ref = f32[8,16,1024]{2,1,0:T(8,128)S(1)} async-done(((f32[8,16,1024]{2,1,0:T(8,128)}), f32[8,16,1024]{2,1,0:T(8,128)S(1)}, u32[]{:S(2)}, u32[]{:S(2)}) %all-to-all-start.5) | async-done | bytes 524320 | tf_op jit(solution)/shard_map/window/all_to_all | solution.py:25
  150.5 0.8 window.5
  151.3 3.5 %all-to-all-start.6 = ((f32[8,16,1024]{2,1,0:T(8,128)}), f32[8,16,1024]{2,1,0:T(8,128)S(1)}, u32[]{:S(2)}, u32[]{:S(2)}) async-start(f32[8,16,1024]{2,1,0:T(8,128)} %window.5), calls=%async_computation.7 | async-start | bytes 1048576 | tf_op jit(solution)/shard_map/window/all_to_all | solution.py:25
  154.9 3.8 %select_maximum_fusion = f32[1024,1024]{0,1:T(8,128)S(1)} fusion(f32[256,256]{0,1:T(8,128)} %bitcast.126, f32[256,256]{0,1:T(8,128)} %convolution_bitcast_fusion.2, f32[256,256]{0,1:T(8,128)} %bitcast.125, f32[256,512]{0,1:T(8,128)S(1)} %broadcast_in_dim.28, f32[256,512]{0,1:T(8,128)S(1)} %copy-done.20, f32[256,256]{0,1:T(8,128)} %bitcast.124, ...), kind=kLoop, calls=%fused_computation | loop fusion | flops 10485760 | bytes 7602176 | tf_op jit(solution)/shard_map/diagonal/concatenate | solution.py:214
  158.7 1.8 %fusion.48.base_ref = f32[16,1024]{1,0:T(8,128)S(1)} fusion(f32[1024,1024]{0,1:T(8,128)S(1)} %select_maximum_fusion, s32[]{:T(128)S(6)} %select_n.55), kind=kOutput, calls=%fused_computation.88 | convolution fusion | flops 100663296 | bytes 4325380 | tf_op jit(solution)/shard_map/diagonal/dot_general | solution.py:19
  160.6 1.6 fusion.36
  162.2 9.0 %all-to-all-done.6.in_ref = f32[8,16,1024]{2,1,0:T(8,128)S(1)} async-done(((f32[8,16,1024]{2,1,0:T(8,128)}), f32[8,16,1024]{2,1,0:T(8,128)S(1)}, u32[]{:S(2)}, u32[]{:S(2)}) %all-to-all-start.6) | async-done | bytes 524320 | tf_op jit(solution)/shard_map/window/all_to_all | solution.py:25
  171.2 0.7 diagonal.1
  (83 shorter events, 4.6 us)
Async XLA Ops:
  7.2 86.3 %copy-start = (bf16[2048,8,1,32]{0,3,2,1:T(8,128)(2,1)S(1)}, bf16[2048,8,1,32]{0,3,2,1:T(8,128)(2,1)}, u32[]{:S(2)}) copy-start(bf16[2048,8,1,32]{0,3,2,1:T(8,128)(2,1)} %param.5) | copy-start | bytes 3145732
  7.2 81.7 %all-gather.2.cloned.1.call-start = ((), (), s32[]{:S(2)}) async-start(), calls=%async_computation.8 | async-start | bytes 2359296 | tf_op jit(solution)/shard_map/gather/all_gather | solution.py:138
  8.3 1.2 copy-start.1
  9.5 0.9 copy-start.5
  10.4 0.8 copy-start.6
  66.0 20.5 %all-to-all-start.2 = ((bf16[8,32,1024]{2,1,0:T(8,128)(2,1)}), bf16[8,32,1024]{2,1,0:T(8,128)(2,1)S(1)}, u32[]{:S(2)}, u32[]{:S(2)}) async-start(bf16[8,32,1024]{2,1,0:T(8,128)(2,1)} %broadcast_in_dim.26), calls=%async_computation.3 | async-start | bytes 1048576 | tf_op jit(solution)/shard_map/column_block/all_to_all | solution.py:25
  73.3 14.4 %collective-permute-start.1 = (bf16[768,384]{1,0:T(8,128)(2,1)S(1)}, bf16[768,384]{1,0:T(8,128)(2,1)}, u32[]{:S(2)}, u32[]{:S(2)}) collective-permute-start(bf16[768,384]{1,0:T(8,128)(2,1)S(1)} %bitcast.115), channel_id=1, source_target_pairs={{0,1},{1,0},{2,3},{3,2},{4,5},{5,4},{6,7},{7,6},{8,9},{9,8},{10,11... | collective-permute-start | bytes 1769480 | tf_op jit(solution)/shard_map/gather/ppermute | solution.py:143
  88.9 3.6 %copy-start.7 = (bf16[768,384]{1,0:T(8,128)(2,1)}, bf16[768,384]{1,0:T(8,128)(2,1)S(1)}, u32[]{:S(2)}) copy-start(bf16[768,384]{1,0:T(8,128)(2,1)S(1)} %get-tuple-element.9) | copy-start | bytes 1769476
  88.9 6.3 %collective-permute-start = (bf16[2048,512]{1,0:T(8,128)(2,1)}, bf16[2048,512]{1,0:T(8,128)(2,1)S(1)}, u32[]{:S(2)}, u32[]{:S(2)}) collective-permute-start(bf16[2048,512]{1,0:T(8,128)(2,1)} %all-gather.2.cloned.1.call-done), channel_id=1, source_target_pairs={{0,1},{1,0},{2,3},{3,2},{4,5},{5,4},{6,7},{7,6},{8,9},{9,8},{10,11... | collective-permute-start | bytes 6291464 | tf_op jit(solution)/shard_map/gather/ppermute | solution.py:142
  90.8 1.7 copy-start.18
  91.6 4.4 %copy-start.12 = (f32[256,256]{1,0:T(8,128)}, f32[256,256]{1,0:T(8,128)S(1)}, u32[]{:S(2)}) copy-start(f32[256,256]{1,0:T(8,128)S(1)} %get-tuple-element.6) | copy-start | bytes 786436
  91.8 4.2 %copy-start.9 = (f32[256,256]{1,0:T(8,128)}, f32[256,256]{1,0:T(8,128)S(1)}, u32[]{:S(2)}) copy-start(f32[256,256]{1,0:T(8,128)S(1)} %convolution_subtract_fusion.2) | copy-start | bytes 786436
  92.0 4.7 %copy-start.17 = (f32[256,256]{1,0:T(8,128)}, f32[256,256]{1,0:T(8,128)S(1)}, u32[]{:S(2)}) copy-start(f32[256,256]{1,0:T(8,128)S(1)} %convolution_subtract_fusion) | copy-start | bytes 786436
  92.0 1.8 copy-start.22
  92.5 4.2 %copy-start.15 = (f32[256,256]{1,0:T(8,128)}, f32[256,256]{1,0:T(8,128)S(1)}, u32[]{:S(2)}) copy-start(f32[256,256]{1,0:T(8,128)S(1)} %fusion) | copy-start | bytes 786436
  96.7 3.3 %copy-start.11 = (f32[256,256]{0,1:T(8,128)}, f32[256,256]{0,1:T(8,128)S(1)}, u32[]{:S(2)}) copy-start(f32[256,256]{0,1:T(8,128)S(1)} %slice_add_fusion.1) | copy-start | bytes 786436
  97.5 2.5 %copy-start.8 = (f32[256,256]{0,1:T(8,128)}, f32[256,256]{0,1:T(8,128)S(1)}, u32[]{:S(2)}) copy-start(f32[256,256]{0,1:T(8,128)S(1)} %slice_add_fusion) | copy-start | bytes 786436
  97.9 2.1 %copy-start.13 = (f32[256,256]{0,1:T(8,128)}, f32[256,256]{0,1:T(8,128)S(1)}, u32[]{:S(2)}) copy-start(f32[256,256]{0,1:T(8,128)S(1)} %convolution_add_fusion.2) | copy-start | bytes 786436
  97.9 2.1 %copy-start.19 = (f32[256,256]{0,1:T(8,128)}, f32[256,256]{0,1:T(8,128)S(1)}, u32[]{:S(2)}) copy-start(f32[256,256]{0,1:T(8,128)S(1)} %slice.146) | copy-start | bytes 786436
  106.8 1.1 copy-start.3
  107.9 21.3 %all-to-all-start.4 = ((f32[4,16,5120]{2,1,0:T(8,128)}), f32[4,16,5120]{2,1,0:T(8,128)S(1)}, u32[]{:S(2)}, u32[]{:S(2)}) async-start(f32[4,16,5120]{2,1,0:T(8,128)} %copy-done.3), calls=%async_computation.5 | async-start | bytes 2621440 | tf_op jit(solution)/shard_map/window/all_to_all | solution.py:25
  112.4 4.9 %copy-start.2 = (f32[4,256,256]{2,1,0:T(8,128)S(1)}, f32[4,256,256]{2,1,0:T(8,128)}, u32[]{:S(2)}) copy-start(f32[4,256,256]{2,1,0:T(8,128)} %t_ref.1) | copy-start | bytes 3145732
  112.4 48.2 %reduce-scatter.2.cloned.1.call-start = ((), (), s32[]{:S(2)}) async-start(), calls=%async_computation.9 | async-start | bytes 1179648 | tf_op jit(solution)/shard_map/cross/reduce_scatter | solution.py:180
  129.2 0.8 copy-start.4
  130.0 8.3 %copy-start.10 = (f32[256,256]{1,0:T(8,128)S(1)}, f32[256,256]{1,0:T(8,128)}, u32[]{:S(2)}) copy-start(f32[256,256]{1,0:T(8,128)} %copy-done.9) | copy-start | bytes 786436
  130.0 8.3 %copy-start.16 = (f32[256,256]{1,0:T(8,128)S(1)}, f32[256,256]{1,0:T(8,128)}, u32[]{:S(2)}) copy-start(f32[256,256]{1,0:T(8,128)} %copy-done.15) | copy-start | bytes 786436
  130.0 8.3 %copy-start.21 = (f32[256,256]{1,0:T(8,128)S(1)}, f32[256,256]{1,0:T(8,128)}, u32[]{:S(2)}) copy-start(f32[256,256]{1,0:T(8,128)} %get-tuple-element.16) | copy-start | bytes 786436
  130.0 20.5 %all-to-all-start.5 = ((f32[8,16,1024]{2,1,0:T(8,128)}), f32[8,16,1024]{2,1,0:T(8,128)S(1)}, u32[]{:S(2)}, u32[]{:S(2)}) async-start(f32[8,16,1024]{2,1,0:T(8,128)} %copy-done.4), calls=%async_computation.6 | async-start | bytes 1048576 | tf_op jit(solution)/shard_map/window/all_to_all | solution.py:25
  140.1 14.8 %copy-start.14 = (f32[256,768]{0,1:T(8,128)S(1)}, f32[256,768]{0,1:T(8,128)}, u32[]{:S(2)}) copy-start(f32[256,768]{0,1:T(8,128)} %convolution_bitcast_fusion) | copy-start | bytes 2359300
  140.1 14.8 %copy-start.20 = (f32[256,512]{0,1:T(8,128)S(1)}, f32[256,512]{0,1:T(8,128)}, u32[]{:S(2)}) copy-start(f32[256,512]{0,1:T(8,128)} %convolution_bitcast_fusion.1) | copy-start | bytes 1572868
  151.3 19.9 %all-to-all-start.6 = ((f32[8,16,1024]{2,1,0:T(8,128)}), f32[8,16,1024]{2,1,0:T(8,128)S(1)}, u32[]{:S(2)}, u32[]{:S(2)}) async-start(f32[8,16,1024]{2,1,0:T(8,128)} %window.5), calls=%async_computation.7 | async-start | bytes 1048576 | tf_op jit(solution)/shard_map/window/all_to_all | solution.py:25
Sparse Core Ops, SparseCore 0:
  32.5 50.9 all-gather.1
  117.5 34.0 reduce-scatter.1

commit v3 on v2

v3 whole, which is shorter than its diff:
```python
import jax
import jax.numpy as jnp
from jax import lax
from jax.experimental import pallas as pl
from jax.experimental.pallas import tpu as pltpu
from jax.sharding import Mesh, PartitionSpec as P

HIGHEST = lax.Precision.HIGHEST
HIGH = lax.Precision.HIGH
BF16 = jnp.bfloat16
F32 = jnp.float32


def mm(a, b, precision=HIGH):
    return jnp.dot(a, b, precision=precision, preferred_element_type=F32)


def exchange(x, axis):
    return lax.all_to_all(x, axis, 0, 0, tiled=True)


def gather(x, axis, size):
    return exchange(jnp.broadcast_to(x[None], (size,) + x.shape), axis)


def local_call(kernel, shapes, scalars, *arrays, scratch=()):
    vmem = pl.BlockSpec(memory_space=pltpu.VMEM)
    smem = pl.BlockSpec(memory_space=pltpu.SMEM)
    return pl.pallas_call(
        kernel,
        out_shape=shapes,
        in_specs=[smem] * len(scalars) + [vmem] * len(arrays),
        out_specs=jax.tree.map(lambda _: vmem, shapes),
        scratch_shapes=[pltpu.VMEM(*each) for each in scratch],
        compiler_params=pltpu.CompilerParams(vmem_limit_bytes=24 * 1024 * 1024),
    )(*scalars, *arrays)


def panel_kernel(structure_ref, place_ref, a_ref, w_ref, t_ref, message_ref, panel_ref):
    supernodes, width = t_ref.shape[0], t_ref.shape[1]
    local, wlocal = a_ref.shape[0], w_ref.shape[0]
    ha = supernodes * width // 2
    hw = (supernodes - 1) * width // 2
    for h in range(2):
        message_ref[h, local:, hw:] = jnp.zeros((wlocal, ha - hw), BF16)
    for j in range(supernodes):
        at = slice(j * width, (j + 1) * width)
        rows = jnp.concatenate([a_ref[:, at], w_ref[:, at]], axis=0)
        product = mm(rows, t_ref[j], HIGHEST)
        scale = structure_ref[j, place_ref[0]].astype(F32)
        a = (scale * product[:local]).astype(BF16)
        for copy in range(2):
            start = (copy * supernodes + j) * width
            panel_ref[:, start : start + width] = a
        h, off = divmod(j * width, ha)
        message_ref[h, :local, off : off + width] = a
        if j == 0:
            continue
        scale = jnp.where(place_ref[1] < j, 1.0, 0.0)
        w = (scale * product[local:]).astype(BF16)
        for half in range(2):
            message_ref[half, local:, (j - 1) * width // 2 : j * width // 2] = w[
                :, half * width // 2 : (half + 1) * width // 2
            ]


def pack_kernel(got_ref, out_ref):
    blocks, height, columns = got_ref.shape
    rows = (out_ref.shape[0] - 96) // blocks
    edge = rows * blocks
    half = columns // 4
    for i in range(blocks):
        out_ref[i * rows : (i + 1) * rows] = got_ref[i, :rows]
    for k in range(2):
        for c in range(2):
            at = edge + (2 * k + c) * 16
            block = 2 * k + c
            out_ref[at : at + 16, : 3 * half] = got_ref[block, rows:, : 3 * half]
            out_ref[at : at + 16, 3 * half :] = got_ref[8 + block, rows:, 2 * half : 3 * half]
            at = edge + 64 + c * 16
            out_ref[at : at + 16, 2 * k * half : 2 * (k + 1) * half] = got_ref[
                4 + block, rows:, half : 3 * half
            ]


def split(v):
    high = v.astype(BF16)
    return high, (v - high.astype(F32)).astype(BF16)


def dot(a, b):
    return jnp.dot(a, b, preferred_element_type=F32)


def dot_t(a, b):
    return lax.dot_general(a, b, (((0,), (0,)), ((), ())), preferred_element_type=F32)


def product_kernel(x_ref, sigma_ref, p0_ref, p1_ref, p2_ref, p3_ref, out_ref, held_ref):
    nz, nx, rows, columns = held_ref.shape
    for shift, ref in enumerate((p0_ref, p1_ref, p2_ref, p3_ref)):
        source = lax.rem(x_ref[0] + nx - shift, nx)
        for i in range(nz):
            held_ref[i, source] = ref[i * rows : (i + 1) * rows]
    out_ref[...] = dot(sigma_ref[...], held_ref[...].reshape(nz * nx * rows, columns))


def inverse_kernel(core_ref, x_ref, *refs):
    pieces, (high_ref, low_ref, held_ref) = refs[:8], refs[8:]
    width = high_ref.shape[0] // 3
    half = width // 2
    nx = held_ref.shape[3]
    edge = pieces[0].shape[0] - 96
    for group in range(2):
        side = core_ref[0] if group == 0 else 1 - core_ref[0]
        for shift in range(nx):
            ref = pieces[group * nx + shift]
            source = lax.rem(x_ref[0] + nx - shift, nx)
            for k in range(2):
                at = slice(edge + k * 32, edge + (k + 1) * 32)
                held_ref[side, 0, k, source] = ref[at, : 3 * half]
                held_ref[side, 1, k, source, :, half:] = ref[
                    edge + 64 : edge + 96, 2 * k * half : 2 * (k + 1) * half
                ]
                held_ref[side, 2, k, source, :, 2 * half :] = ref[at, 3 * half :]
    w = lambda i, j: jnp.concatenate(
        [
            held_ref[side, i, :, :, :, (j - 1) * half : j * half].reshape(width, half)
            for side in range(2)
        ],
        axis=1,
    )
    f = lambda i, j: w(i, j).astype(F32)
    u = {(i, i + 1): -f(i, i + 1) for i in range(3)}
    u[0, 2] = dot(w(0, 1), w(1, 2)) - f(0, 2)
    u[1, 3] = dot(w(1, 2), w(2, 3)) - f(1, 3)
    high, low = split(u[0, 2])
    u[0, 3] = dot(w(0, 1), w(1, 3)) - f(0, 3) - dot(high, w(2, 3)) - dot(low, w(2, 3))
    for i in range(3):
        for j in range(1, 4):
            at = (slice(i * width, (i + 1) * width), slice((j - 1) * width, j * width))
            value = u.get((i, j))
            value = jnp.zeros((width, width), F32) if value is None else value
            high_ref[at], low_ref[at] = split(value)


def left_kernel(panel_ref, high_ref, low_ref, lh_ref, ll_ref):
    width = lh_ref.shape[1] // 4
    lh_ref[:, :width] = panel_ref[:, :width]
    ll_ref[:, :width] = jnp.zeros((panel_ref.shape[0], width), BF16)
    for j in range(1, 4):
        a = panel_ref[:, : j * width]
        at = (slice(0, j * width), slice((j - 1) * width, j * width))
        value = panel_ref[:, j * width : (j + 1) * width].astype(F32)
        value = value + dot(a, high_ref[at]) + dot(a, low_ref[at])
        cut = slice(j * width, (j + 1) * width)
        lh_ref[:, cut], ll_ref[:, cut] = split(value)


def window_kernel(
    core_ref, mine_ref, other_ref, high_ref, low_ref, lh_ref, ll_ref,
    right_ref, keep_ref, send_ref, packed_ref, rh_ref, rl_ref, fh_ref, fl_ref,
):
    nc, nx, rows, _ = packed_ref.shape
    size, window = rh_ref.shape
    width = window // 4
    first = core_ref[0] == 0
    ny, local = right_ref.shape[0], right_ref.shape[1]
    fs = []
    for h in range(2):
        a, b = (mine_ref, other_ref) if h == 0 else (other_ref, mine_ref)
        value = jnp.where(first, a[...], b[...])
        at = slice(h * window // 2, (h + 1) * window // 2)
        fh_ref[:, at], fl_ref[:, at] = split(value)
        fs += [value[:, :width], value[:, width:]]
    for j in range(4):
        value = fs[j]
        if j:
            at = (slice(0, j * width), slice((j - 1) * width, j * width))
            fh = fh_ref[:, : j * width]
            value = value + (
                dot(fh, high_ref[at]) + dot(fl_ref[:, : j * width], high_ref[at]) + dot(fh, low_ref[at])
            )
        cut = slice(j * width, (j + 1) * width)
        for i in range(ny):
            right_ref[i, :, cut] = value[i * local : (i + 1) * local]
        rh_ref[:, cut], rl_ref[:, cut] = split(value)
    at = 0
    for t in range(4):
        n = window - t * width
        cut = slice(t * width, (t + 1) * width)
        lh, ll = lh_ref[:, cut], ll_ref[:, cut]
        rh, rl = rh_ref[:, t * width :], rl_ref[:, t * width :]
        part = dot_t(lh, rh) + dot_t(ll, rh) + dot_t(lh, rl)
        for k in range(2):
            for i in range(nx):
                for c in range(nc):
                    row = ((k * nx + i) * nc + c) * rows
                    packed_ref[c, i, :, at : at + n] = part[row : row + rows]
            at += n
    keep_ref[...] = packed_ref[core_ref[0]]
    send_ref[...] = packed_ref[1 - core_ref[0]]


def exponent(v):
    top = jnp.max(jnp.abs(v), axis=(0, 1), keepdims=True)
    return jnp.floor(jnp.log2(jnp.maximum(top, 1e-30))) - 13.0


def sum_kernel(a_ref, b_ref, out_ref):
    nx, rows, n = a_ref.shape
    for i in range(nx):
        total = a_ref[i] + b_ref[i]
        power = exponent(total)
        out_ref[i, :, :n] = total * jnp.exp2(-power)
        out_ref[i, :, n:] = jnp.broadcast_to(power, (rows, out_ref.shape[2] - n))


def spread_kernel(in_ref, out_ref):
    size, rows, window = out_ref.shape[0], out_ref.shape[1], out_ref.shape[2] - 128
    width = window // 4
    last = in_ref.shape[2] - 128
    scales = [jnp.exp2(in_ref[k, :, last : last + 1]) for k in range(in_ref.shape[0])]
    at = 0
    for i in range(size):
        edge = (i // 2) * width
        n = window - edge
        total = in_ref[0, :, at : at + n] * scales[0]
        for k in range(1, in_ref.shape[0]):
            total = total + in_ref[k, :, at : at + n] * scales[k]
        power = exponent(total)
        if edge:
            out_ref[i, :, :edge] = jnp.zeros((rows, edge), F32)
        out_ref[i, :, edge:window] = total * jnp.exp2(-power)
        out_ref[i, :, window:] = jnp.broadcast_to(power, (rows, 128))
        at += n


def repeat_kernel(in_ref, out_ref):
    window = out_ref.shape[1] - 128
    total = jnp.zeros((out_ref.shape[0], window), F32)
    for i in range(in_ref.shape[0]):
        total = total + in_ref[i, :, :window] * jnp.exp2(in_ref[i, :, window : window + 1])
    power = exponent(total)
    out_ref[:, :window] = total * jnp.exp2(-power)
    out_ref[:, window:] = jnp.broadcast_to(power, (out_ref.shape[0], 128))


def finish_kernel(tile_ref, in_ref, base_ref, out_ref):
    total = base_ref[...]
    window = total.shape[1]
    for i in range(in_ref.shape[0]):
        total = total + in_ref[i, :, :window] * jnp.exp2(in_ref[i, :, window : window + 1])
    columns = lax.broadcasted_iota(jnp.int32, total.shape, 1)
    out_ref[...] = jnp.where(columns >= tile_ref[0] * (window // 4), total, 0.0)


def base_kernel(place_ref, t_ref, high_ref, low_ref, out_ref, vh_ref, vl_ref, rows_ref):
    n, width = t_ref.shape[0], t_ref.shape[1]
    for k in range(n):
        th, tl = split(t_ref[k])
        down = slice(k * width, (k + 1) * width)
        for j in range(n):
            if j < k:
                zero = jnp.zeros((width, width), BF16)
                vh_ref[j, down], vl_ref[j, down] = zero, zero
            elif j == k:
                vh_ref[j, down], vl_ref[j, down] = th, tl
            else:
                at = (down, slice((j - 1) * width, j * width))
                value = dot(th, high_ref[at]) + dot(tl, high_ref[at]) + dot(th, low_ref[at])
                vh_ref[j, down], vl_ref[j, down] = split(value)
    ah, al = vh_ref[place_ref[1]], vl_ref[place_ref[1]]
    for j in range(n):
        vh, vl = vh_ref[j], vl_ref[j]
        rows_ref[:, j * width : (j + 1) * width] = dot_t(ah, vh) + dot_t(al, vh) + dot_t(ah, vl)
    rows = out_ref.shape[0]
    out_ref[...] = rows_ref[pl.ds(pl.multiple_of(place_ref[2] * rows, rows), rows)]


def body(sigma_top, ancestor_rows, window_rows, tile_inverse, structure):
    ny, nz, nx, nc = 8, 8, 4, 2
    supernodes, width = tile_inverse.shape[0], tile_inverse.shape[1]
    window = supernodes * width
    local = ancestor_rows.shape[0]
    wlocal = window_rows.shape[0]
    y, z, x, c = (lax.axis_index(name) for name in ("y", "z", "x", "c"))
    col = (z * nx + x) * nc + c
    tile = ((y * (nz * nx * nc) + col) * local) // width
    wtile = (col * wlocal) // width
    select = lax.dynamic_slice_in_dim(structure, tile, 1, 1)[:, 0].astype(F32)

    with jax.named_scope("panels"):
        ha, hw = window // 2, (window - width) // 2
        place = jnp.stack([tile, wtile, col % (width // wlocal)])
        message, panel = local_call(
            panel_kernel,
            (
                jax.ShapeDtypeStruct((nc, local + wlocal, ha), BF16),
                jax.ShapeDtypeStruct((local, 2 * window), BF16),
            ),
            (structure, place),
            ancestor_rows,
            window_rows,
            tile_inverse,
        )

    shape = lambda *dims, dtype=F32: jax.ShapeDtypeStruct(dims, dtype)
    with jax.named_scope("column_block"):
        panel_c = lax.all_gather(panel, "y", axis=0, tiled=True)

    with jax.named_scope("gather"):
        got = exchange(message, "c").reshape(nc, local + wlocal, ha)
        got = lax.all_gather(got, "z", axis=0, tiled=True)
        swap = [(0, 1), (1, 0)]
        first = local_call(
            pack_kernel, shape(nz * nc * local + 96, ha, dtype=BF16), (), got
        )
        pieces = [first]
        for step in range(1, nx):
            pieces.append(
                lax.ppermute(first, "x", [(i, (i + step) % nx) for i in range(nx)])
            )
        others = [lax.ppermute(piece, "c", swap) for piece in pieces]

    with jax.named_scope("unit_inverse"):
        core = c.reshape(1)
        n = window - width
        high, low = local_call(
            inverse_kernel,
            (shape(n, n, dtype=BF16), shape(n, n, dtype=BF16)),
            (core, x.reshape(1)),
            *pieces,
            *others,
            scratch=(((2, supernodes - 1, 2, nx, 2 * wlocal, n // 2), BF16),),
        )
        lh, ll = local_call(
            left_kernel,
            (shape(ny * local, window, dtype=BF16),) * 2,
            (),
            panel_c,
            high,
            low,
        )

    with jax.named_scope("product"):
        sigma = sigma_top.transpose(1, 2, 3, 0).reshape(ny * local, -1)
        held = (((nz, nx, nc * local, ha), BF16),)
        product = lambda parts: local_call(
            product_kernel,
            shape(ny * local, ha),
            (x.reshape(1),),
            sigma,
            *parts,
            scratch=held,
        )
        own = product(pieces)
        away = product(others)

    with jax.named_scope("window"):
        half = ((ny * local, window), BF16)
        packed = (nx, wlocal, 2 * 10 * width)
        right, keep, send = local_call(
            window_kernel,
            (shape(ny, local, window), shape(*packed), shape(*packed)),
            (core,),
            own,
            away,
            high,
            low,
            lh,
            ll,
            scratch=(((nc,) + packed, F32), half, half, half, half),
        )
        cross = lax.psum_scatter(right, "y", scatter_dimension=0, tiled=True)
        scale = jnp.repeat(select, width)[None, :]
        cross = -(scale * cross.reshape(local, window))
        came = lax.ppermute(send, "c", swap)
        half_type = jnp.float16
        n = packed[-1] + 128
        parts = local_call(sum_kernel, shape(nx, wlocal, n), (), keep, came)
        parts = exchange(parts.astype(half_type), "x").astype(F32)
        spread = local_call(spread_kernel, shape(nz, wlocal, window + 128), (), parts)
        spread = exchange(spread.astype(half_type), "z").astype(F32)
        spread = local_call(repeat_kernel, shape(wlocal, window + 128), (), spread)
        spread = gather(spread.astype(half_type), "y", ny).astype(F32)

    with jax.named_scope("diagonal"):
        spare = ((supernodes, window, width), BF16)
        base = local_call(
            base_kernel,
            shape(wlocal, window),
            (place,),
            tile_inverse,
            high,
            low,
            scratch=(spare, spare, ((width, window), F32)),
        )
        block = local_call(
            finish_kernel, shape(wlocal, window), (wtile.reshape(1),), spread, base
        )
    return cross, block


def solution(mesh):
    fine = Mesh(mesh.devices.reshape(8, 8, 4, 2), ("y", "z", "x", "c"))
    col = ("z", "x", "c")
    return jax.shard_map(
        body,
        mesh=fine,
        in_specs=(P("y", None, col, None), P(("y",) + col, None), P(col, None), P(), P()),
        out_specs=(P(("y",) + col, None), P(col, None)),
        check_vma=False,
    )
```

time: 180 us -> 159 us (0.88)
  matrix products: 15.4 us -> 0 us
  Pallas kernels: 2.94 us -> 14.3 us
  waiting for transfers between devices: 35.1 us -> 24.6 us
  local copies, waits for them, and re-layouts: 18.2 us -> 9.04 us
  other arithmetic: 11.9 us -> 3.08 us
  blocking collectives: 57.7 us -> 66.1 us
  starting transfers between devices: 22.9 us -> 26.9 us
    all_to_all x4 -> x1, waiting for transfers between devices: 34.4 us -> 5.81 us  [exchange(): return lax.all_to_all(x, axis, 0, 0, tiled=True)]
    ppermute x2 -> x8, waiting for transfers between devices: 0.61 us -> 18.7 us  [the longest x3 14.4 us: body(): lax.ppermute(first, 'x', [(i, (i + step) % nx) for i in range(nx)])]
    all_gather x1, blocking collectives: 15.3 us -> 32.5 us  [body(): got = lax.all_gather(got, 'z', axis=0, tiled=True)]
    ppermute x2 -> x8, starting transfers between devices: 3.84 us -> 20.2 us  [the longest x3 10.5 us: body(): lax.ppermute(first, 'x', [(i, (i + step) % nx) for i in range(nx)])]
    dot_general x20 -> x0, matrix products: 15.4 us -> none  [the longest x15 11.2 us: mm(): return jnp.dot(a, b, precision=precision, preferred_element_type=F32)]
    all_to_all x4 -> x1, starting transfers between devices: 19 us -> 6.65 us  [exchange(): return lax.all_to_all(x, axis, 0, 0, tiled=True)]
    pallas_call x5 -> x12, Pallas kernels: 2.94 us -> 14.3 us  [local_call(): pl.pallas_call(kernel, out_shape=shapes, in_specs=[smem] * len(scalars) +...]
    all_to_all x3, blocking collectives: 42.3 us -> 33.5 us  [exchange(): return lax.all_to_all(x, axis, 0, 0, tiled=True)]
  transfers between devices with their start and end apart: 8 -> 11, of which waited for: 5 -> 6; matrix products, arithmetic and copies ran while one was open for 19% -> 2% of each run, Pallas kernels for 1% -> 5%
where the time goes in v3:
time: 159 us; the launch traced here: 158 us
  blocking collectives  66.1 us (42%)
  starting transfers between devices  26.9 us (17%)
  waiting for transfers between devices  24.6 us (15%)
  Pallas kernels  14.3 us (9%)
  between operations  14.3 us (9%)
  local copies, waits for them, and re-layouts  9.04 us (6%)
  other arithmetic  3.08 us (2%)
    all_to_all x3, blocking collectives, exchange(): return lax.all_to_all(x, axis, 0, 0, tiled=True)  33.5 us
    all_gather x1, blocking collectives, body(): got = lax.all_gather(got, 'z', axis=0, tiled=True)  32.5 us
    ppermute x3, waiting for transfers between devices, body(): lax.ppermute(first, 'x', [(i, (i + step) % nx) for i in range(nx)])  14.4 us
    pallas_call x12, Pallas kernels, local_call(): pl.pallas_call(kernel, out_shape=shapes, in_specs=[smem] * len(scalars) +...  14.3 us
    ppermute x3, starting transfers between devices, body(): lax.ppermute(first, 'x', [(i, (i + step) % nx) for i in range(nx)])  10.5 us
    unnamed x24, local copies, waits for them, and re-layouts  8.29 us
    ppermute x4, starting transfers between devices, body(): others = [lax.ppermute(piece, 'c', swap) for piece in pieces]  7.65 us
    all_to_all x1, starting transfers between devices, exchange(): return lax.all_to_all(x, axis, 0, 0, tiled=True)  6.65 us
  transfers between devices with their start and end apart: 11, of which 6 were waited for; matrix products, arithmetic and copies ran while one was open for 2% of the time, Pallas kernels for 5%

profile of v3, /device:TPU:2, one launch (start us, length us, event | category | flops | bytes accessed | tf_op | source)
XLA Modules:
  0.0 158.3 jit_solution(11760260384581127035)
XLA Ops:
  7.2 0.0 all-gather.2.cloned.1.call-start
  7.3 0.1 pad_add_fusion.place_ref
  7.3 1.2 copy-done
  8.6 0.9 copy-done.7
  9.5 0.8 copy-done.8
  10.3 0.7 copy-done.9
  11.0 1.9 %panels.1 = (bf16[2,48,512]{2,1,0:T(8,128)(2,1)S(1)}, bf16[32,2048]{1,0:T(8,128)(2,1)}) custom-call(s32[4,64]{1,0:T(4,128)S(1)} %copy-done.9, s32[3]{0:T(128)S(1)} %pad_add_fusion.place_ref, f32[32,1024]{1,0:T(8,128)S(1)} %copy-done.7, f32[16,1024]{1,0:T(8,128)S(1)} %copy-done.8, f32[4,256,256]{2,1,0:T(8,128)S(1)} %copy-done), custom_call_target="tpu_custom_call" | custom-call | tf_op jit(solution)/shard_map/panels/pallas_call | solution.py:29
  12.9 0.0 reduce-scatter.2.cloned.1.call-start
  13.0 3.9 %all_to_all.20 = bf16[2,48,512]{2,1,0:T(8,128)(2,1)S(1)} all-to-all(bf16[2,48,512]{2,1,0:T(8,128)(2,1)S(1)} %get-tuple-element.11), channel_id=1, replica_groups=mesh['y'=8,'z'=8,'x'=4,'c'=2] {'c'}, dimensions={0} | all-to-all | bytes 196608 | tf_op jit(solution)/shard_map/gather/all_to_all | solution.py:19
  16.9 32.5 %all_gather.6.got_ref = bf16[16,48,512]{2,1,0:T(8,128)(2,1)S(1)} all-gather(bf16[2,48,512]{2,1,0:T(8,128)(2,1)S(1)} %all_to_all.20), channel_id=1, replica_groups=mesh['y'=8,'z'=8,'x'=4,'c'=2] {'z'}, dimensions={0}, use_global_device_ids=true | all-gather | bytes 884736 | tf_op jit(solution)/shard_map/gather/all_gather | solution.py:314
  49.5 3.4 %collective-permute-start = (bf16[608,512]{1,0:T(8,128)(2,1)S(1)}, bf16[608,512]{1,0:T(8,128)(2,1)S(1)}, u32[]{:S(2)}, u32[]{:S(2)}) collective-permute-start(bf16[608,512]{1,0:T(8,128)(2,1)S(1)} %gather.1.p0_ref.refs_0_), channel_id=1, source_target_pairs={{0,2},{2,4},{4,6},{6,0},{1,3},{3,5},{5,7},{7,1},{8,10},{10,12},{12... | collective-permute-start | bytes 1867784 | tf_op jit(solution)/shard_map/gather/ppermute | solution.py:322
  52.9 3.0 %collective-permute-start.1 = (bf16[608,512]{1,0:T(8,128)(2,1)S(1)}, bf16[608,512]{1,0:T(8,128)(2,1)S(1)}, u32[]{:S(2)}, u32[]{:S(2)}) collective-permute-start(bf16[608,512]{1,0:T(8,128)(2,1)S(1)} %gather.1.p0_ref.refs_0_), channel_id=1, source_target_pairs={{0,4},{2,6},{4,0},{6,2},{1,5},{3,7},{5,1},{7,3},{8,12},{10,14},{12... | collective-permute-start | bytes 1867784 | tf_op jit(solution)/shard_map/gather/ppermute | solution.py:322
  55.9 4.1 %collective-permute-start.2 = (bf16[608,512]{1,0:T(8,128)(2,1)S(1)}, bf16[608,512]{1,0:T(8,128)(2,1)S(1)}, u32[]{:S(2)}, u32[]{:S(2)}) collective-permute-start(bf16[608,512]{1,0:T(8,128)(2,1)S(1)} %gather.1.p0_ref.refs_0_), channel_id=1, source_target_pairs={{0,6},{2,0},{4,2},{6,4},{1,7},{3,1},{5,3},{7,5},{8,14},{10,8},{12,... | collective-permute-start | bytes 1867784 | tf_op jit(solution)/shard_map/gather/ppermute | solution.py:322
  60.0 1.9 %collective-permute-start.3 = (bf16[608,512]{1,0:T(8,128)(2,1)S(1)}, bf16[608,512]{1,0:T(8,128)(2,1)S(1)}, u32[]{:S(2)}, u32[]{:S(2)}) collective-permute-start(bf16[608,512]{1,0:T(8,128)(2,1)S(1)} %gather.1.p0_ref.refs_0_), channel_id=1, source_target_pairs={{0,1},{1,0},{2,3},{3,2},{4,5},{5,4},{6,7},{7,6},{8,9},{9,8},{10,11... | collective-permute-start | bytes 1867784 | tf_op jit(solution)/shard_map/gather/ppermute | solution.py:324
  61.9 6.4 %collective-permute-done.p1_ref.refs_1_ = bf16[608,512]{1,0:T(8,128)(2,1)S(1)} collective-permute-done((bf16[608,512]{1,0:T(8,128)(2,1)S(1)}, bf16[608,512]{1,0:T(8,128)(2,1)S(1)}, u32[]{:S(2)}, u32[]{:S(2)}) %collective-permute-start) | collective-permute-done | bytes 622624 | tf_op jit(solution)/shard_map/gather/ppermute | solution.py:322
  68.4 1.9 %collective-permute-start.4 = (bf16[608,512]{1,0:T(8,128)(2,1)S(1)}, bf16[608,512]{1,0:T(8,128)(2,1)S(1)}, u32[]{:S(2)}, u32[]{:S(2)}) collective-permute-start(bf16[608,512]{1,0:T(8,128)(2,1)S(1)} %collective-permute-done.p1_ref.refs_1_), channel_id=1, source_target_pairs={{0,1},{1,0},{2,3},{3,2},{4,5},{5,4},{6,7},{7,6},{8,9},{9,8},{10,11... | collective-permute-start | bytes 1867784 | tf_op jit(solution)/shard_map/gather/ppermute | solution.py:324
  70.3 3.0 %collective-permute-done.1.p2_ref.refs_2_ = bf16[608,512]{1,0:T(8,128)(2,1)S(1)} collective-permute-done((bf16[608,512]{1,0:T(8,128)(2,1)S(1)}, bf16[608,512]{1,0:T(8,128)(2,1)S(1)}, u32[]{:S(2)}, u32[]{:S(2)}) %collective-permute-start.1) | collective-permute-done | bytes 622624 | tf_op jit(solution)/shard_map/gather/ppermute | solution.py:322
  73.3 1.9 %collective-permute-start.5 = (bf16[608,512]{1,0:T(8,128)(2,1)S(1)}, bf16[608,512]{1,0:T(8,128)(2,1)S(1)}, u32[]{:S(2)}, u32[]{:S(2)}) collective-permute-start(bf16[608,512]{1,0:T(8,128)(2,1)S(1)} %collective-permute-done.1.p2_ref.refs_2_), channel_id=1, source_target_pairs={{0,1},{1,0},{2,3},{3,2},{4,5},{5,4},{6,7},{7,6},{8,9},{9,8},{10,11... | collective-permute-start | bytes 1867784 | tf_op jit(solution)/shard_map/gather/ppermute | solution.py:324
  75.2 5.0 %collective-permute-done.2.p3_ref.refs_3_ = bf16[608,512]{1,0:T(8,128)(2,1)S(1)} collective-permute-done((bf16[608,512]{1,0:T(8,128)(2,1)S(1)}, bf16[608,512]{1,0:T(8,128)(2,1)S(1)}, u32[]{:S(2)}, u32[]{:S(2)}) %collective-permute-start.2) | collective-permute-done | bytes 622624 | tf_op jit(solution)/shard_map/gather/ppermute | solution.py:322
  80.2 1.9 %collective-permute-start.6 = (bf16[608,512]{1,0:T(8,128)(2,1)S(1)}, bf16[608,512]{1,0:T(8,128)(2,1)S(1)}, u32[]{:S(2)}, u32[]{:S(2)}) collective-permute-start(bf16[608,512]{1,0:T(8,128)(2,1)S(1)} %collective-permute-done.2.p3_ref.refs_3_), channel_id=1, source_target_pairs={{0,1},{1,0},{2,3},{3,2},{4,5},{5,4},{6,7},{7,6},{8,9},{9,8},{10,11... | collective-permute-start | bytes 1867784 | tf_op jit(solution)/shard_map/gather/ppermute | solution.py:324
  82.1 0.8 product.2.mine_ref
  83.0 1.1 collective-permute-done.6.p3_ref.refs_7_
  84.1 0.8 product.3.other_ref
  84.9 0.5 unit_inverse.2
  85.5 1.2 copy-done.5
  86.7 0.6 unit_inverse.3
  87.3 3.4 %window.4 = (f32[8,32,1024]{2,1,0:T(8,128)S(1)}, f32[4,16,5120]{2,1,0:T(8,128)S(1)}, f32[4,16,5120]{2,1,0:T(8,128)}) custom-call(s32[1]{0:T(128)} %bitcast.core_ref, f32[256,512]{1,0:T(8,128)S(1)} %product.2.mine_ref, f32[256,512]{1,0:T(8,128)S(1)} %product.3.other_ref, bf16[768,768]{1,0:T(8,128)(2,1)S(1)} %get-tuple-element.12.high_ref, ...), custom_call_target="tpu_custom_call" | custom-call | tf_op jit(solution)/shard_map/window/pallas_call | solution.py:29
  90.7 1.1 copy-done.3
  91.8 1.0 copy-done.6
  92.7 2.0 %collective-permute-start.7 = (f32[4,16,5120]{2,1,0:T(8,128)}, f32[4,16,5120]{2,1,0:T(8,128)}, u32[]{:S(2)}, u32[]{:S(2)}) collective-permute-start(f32[4,16,5120]{2,1,0:T(8,128)} %get-tuple-element.19), channel_id=1, source_target_pairs={{0,1},{1,0},{2,3},{3,2},{4,5},{5,4},{6,7},{7,6},{8,9},{9,8},{10,11... | collective-permute-start | bytes 3932168 | tf_op jit(solution)/shard_map/window/ppermute | solution.py:378
  94.8 3.2 %collective-permute-done.7.b_ref = f32[4,16,5120]{2,1,0:T(8,128)} collective-permute-done((f32[4,16,5120]{2,1,0:T(8,128)}, f32[4,16,5120]{2,1,0:T(8,128)}, u32[]{:S(2)}, u32[]{:S(2)}) %collective-permute-start.7) | collective-permute-done | bytes 1310752 | tf_op jit(solution)/shard_map/window/ppermute | solution.py:378
  98.0 1.3 copy-done.4
  99.3 1.7 %window.5 = f32[4,16,5248]{2,1,0:T(8,128)S(1)} custom-call(f32[4,16,5120]{2,1,0:T(8,128)S(1)} %copy-done.4, f32[4,16,5120]{2,1,0:T(8,128)} %collective-permute-done.7.b_ref), custom_call_target="tpu_custom_call" | custom-call | tf_op jit(solution)/shard_map/window/pallas_call | solution.py:29
  101.0 0.1 convert_element_type.26
  101.0 13.6 %all_to_all.21 = f16[4,16,5248]{2,1,0:T(8,128)(2,1)S(1)} all-to-all(f16[4,16,5248]{2,1,0:T(8,128)(2,1)S(1)} %convert_element_type.26), channel_id=1, replica_groups=mesh['y'=8,'z'=8,'x'=4,'c'=2] {'x'}, dimensions={0} | all-to-all | bytes 1343488 | tf_op jit(solution)/shard_map/window/all_to_all | solution.py:19
  114.7 0.1 convert_element_type.27.in_ref
  114.8 0.3 window.6
  115.1 16.0 %all_to_all.22 = f16[8,16,1152]{2,1,0:T(8,128)(2,1)S(1)} all-to-all(f16[8,16,1152]{2,1,0:T(8,128)(2,1)S(1)} %convert_element_type.28), channel_id=1, replica_groups=mesh['y'=8,'z'=8,'x'=4,'c'=2] {'z'}, dimensions={0} | all-to-all | bytes 589824 | tf_op jit(solution)/shard_map/window/all_to_all | solution.py:19
  131.1 0.2 window.7
  131.4 0.7 broadcast_in_dim.10
  132.1 6.6 %all-to-all-start.3 = ((f16[8,16,1152]{2,1,0:T(8,128)(2,1)}), f16[8,16,1152]{2,1,0:T(8,128)(2,1)}, u32[]{:S(2)}, u32[]{:S(2)}) async-start(f16[8,16,1152]{2,1,0:T(8,128)(2,1)} %broadcast_in_dim.10), calls=%async_computation.4 | async-start | bytes 589824 | tf_op jit(solution)/shard_map/window/all_to_all | solution.py:19
  138.8 0.2 convert_reduce_fusion
  139.0 0.1 broadcast_bitcast_fusion
  139.0 3.2 %diagonal.2.base_ref = f32[16,1024]{1,0:T(8,128)S(1)} custom-call(s32[3]{0:T(128)S(1)} %pad_add_fusion.place_ref, f32[4,256,256]{2,1,0:T(8,128)S(1)} %copy-done.1, bf16[768,768]{1,0:T(8,128)(2,1)S(1)} %get-tuple-element.12.high_ref, bf16[768,768]{1,0:T(8,128)(2,1)S(1)} %get-tuple-element.13.low_ref), custom_call_target="tpu_custom_call" | custom-call | tf_op jit(solution)/shard_map/diagonal/pallas_call | solution.py:29
  142.3 1.6 fusion
  143.9 5.8 %all-to-all-done.3 = f16[8,16,1152]{2,1,0:T(8,128)(2,1)} async-done(((f16[8,16,1152]{2,1,0:T(8,128)(2,1)}), f16[8,16,1152]{2,1,0:T(8,128)(2,1)}, u32[]{:S(2)}, u32[]{:S(2)}) %all-to-all-start.3) | async-done | bytes 294944 | tf_op jit(solution)/shard_map/window/all_to_all | solution.py:19
  149.7 1.0 convert_element_type.31.in_ref
  150.7 0.7 diagonal.3
  (26 shorter events, 0.2 us)
Async XLA Ops:
  7.2 78.3 %all-gather.2.cloned.1.call-start = ((), (), s32[]{:S(2)}) async-start(), calls=%async_computation.5 | async-start | bytes 1179648 | tf_op jit(solution)/shard_map/column_block/all_gather | solution.py:310
  7.3 1.2 copy-start
  8.6 0.9 copy-start.7
  9.5 0.8 copy-start.8
  10.3 0.7 copy-start.9
  12.9 69.2 %copy-start.2 = (bf16[2048,8,1,32]{0,3,2,1:T(8,128)(2,1)S(1)}, bf16[2048,8,1,32]{0,3,2,1:T(8,128)(2,1)}, u32[]{:S(2)}) copy-start(bf16[2048,8,1,32]{0,3,2,1:T(8,128)(2,1)} %param.5) | copy-start | bytes 3145732
  12.9 129.4 %reduce-scatter.2.cloned.1.call-start = ((), (), s32[]{:S(2)}) async-start(), calls=%async_computation.6 | async-start | bytes 1179648 | tf_op jit(solution)/shard_map/window/reduce_scatter | solution.py:375
  49.5 18.9 %collective-permute-start = (bf16[608,512]{1,0:T(8,128)(2,1)S(1)}, bf16[608,512]{1,0:T(8,128)(2,1)S(1)}, u32[]{:S(2)}, u32[]{:S(2)}) collective-permute-start(bf16[608,512]{1,0:T(8,128)(2,1)S(1)} %gather.1.p0_ref.refs_0_), channel_id=1, source_target_pairs={{0,2},{2,4},{4,6},{6,0},{1,3},{3,5},{5,7},{7,1},{8,10},{10,12},{12... | collective-permute-start | bytes 1867784 | tf_op jit(solution)/shard_map/gather/ppermute | solution.py:322
  52.9 20.4 %collective-permute-start.1 = (bf16[608,512]{1,0:T(8,128)(2,1)S(1)}, bf16[608,512]{1,0:T(8,128)(2,1)S(1)}, u32[]{:S(2)}, u32[]{:S(2)}) collective-permute-start(bf16[608,512]{1,0:T(8,128)(2,1)S(1)} %gather.1.p0_ref.refs_0_), channel_id=1, source_target_pairs={{0,4},{2,6},{4,0},{6,2},{1,5},{3,7},{5,1},{7,3},{8,12},{10,14},{12... | collective-permute-start | bytes 1867784 | tf_op jit(solution)/shard_map/gather/ppermute | solution.py:322
  55.9 24.2 %collective-permute-start.2 = (bf16[608,512]{1,0:T(8,128)(2,1)S(1)}, bf16[608,512]{1,0:T(8,128)(2,1)S(1)}, u32[]{:S(2)}, u32[]{:S(2)}) collective-permute-start(bf16[608,512]{1,0:T(8,128)(2,1)S(1)} %gather.1.p0_ref.refs_0_), channel_id=1, source_target_pairs={{0,6},{2,0},{4,2},{6,4},{1,7},{3,1},{5,3},{7,5},{8,14},{10,8},{12,... | collective-permute-start | bytes 1867784 | tf_op jit(solution)/shard_map/gather/ppermute | solution.py:322
  60.0 22.9 %collective-permute-start.3 = (bf16[608,512]{1,0:T(8,128)(2,1)S(1)}, bf16[608,512]{1,0:T(8,128)(2,1)S(1)}, u32[]{:S(2)}, u32[]{:S(2)}) collective-permute-start(bf16[608,512]{1,0:T(8,128)(2,1)S(1)} %gather.1.p0_ref.refs_0_), channel_id=1, source_target_pairs={{0,1},{1,0},{2,3},{3,2},{4,5},{5,4},{6,7},{7,6},{8,9},{9,8},{10,11... | collective-permute-start | bytes 1867784 | tf_op jit(solution)/shard_map/gather/ppermute | solution.py:324
  68.4 14.6 %collective-permute-start.4 = (bf16[608,512]{1,0:T(8,128)(2,1)S(1)}, bf16[608,512]{1,0:T(8,128)(2,1)S(1)}, u32[]{:S(2)}, u32[]{:S(2)}) collective-permute-start(bf16[608,512]{1,0:T(8,128)(2,1)S(1)} %collective-permute-done.p1_ref.refs_1_), channel_id=1, source_target_pairs={{0,1},{1,0},{2,3},{3,2},{4,5},{5,4},{6,7},{7,6},{8,9},{9,8},{10,11... | collective-permute-start | bytes 1867784 | tf_op jit(solution)/shard_map/gather/ppermute | solution.py:324
  73.3 9.7 %collective-permute-start.5 = (bf16[608,512]{1,0:T(8,128)(2,1)S(1)}, bf16[608,512]{1,0:T(8,128)(2,1)S(1)}, u32[]{:S(2)}, u32[]{:S(2)}) collective-permute-start(bf16[608,512]{1,0:T(8,128)(2,1)S(1)} %collective-permute-done.1.p2_ref.refs_2_), channel_id=1, source_target_pairs={{0,1},{1,0},{2,3},{3,2},{4,5},{5,4},{6,7},{7,6},{8,9},{9,8},{10,11... | collective-permute-start | bytes 1867784 | tf_op jit(solution)/shard_map/gather/ppermute | solution.py:324
  80.2 3.9 %collective-permute-start.6 = (bf16[608,512]{1,0:T(8,128)(2,1)S(1)}, bf16[608,512]{1,0:T(8,128)(2,1)S(1)}, u32[]{:S(2)}, u32[]{:S(2)}) collective-permute-start(bf16[608,512]{1,0:T(8,128)(2,1)S(1)} %collective-permute-done.2.p3_ref.refs_3_), channel_id=1, source_target_pairs={{0,1},{1,0},{2,3},{3,2},{4,5},{5,4},{6,7},{7,6},{8,9},{9,8},{10,11... | collective-permute-start | bytes 1867784 | tf_op jit(solution)/shard_map/gather/ppermute | solution.py:324
  85.4 1.2 copy-start.5
  90.7 1.1 copy-start.3
  91.8 1.0 copy-start.6
  92.7 5.3 %collective-permute-start.7 = (f32[4,16,5120]{2,1,0:T(8,128)}, f32[4,16,5120]{2,1,0:T(8,128)}, u32[]{:S(2)}, u32[]{:S(2)}) collective-permute-start(f32[4,16,5120]{2,1,0:T(8,128)} %get-tuple-element.19), channel_id=1, source_target_pairs={{0,1},{1,0},{2,3},{3,2},{4,5},{5,4},{6,7},{7,6},{8,9},{9,8},{10,11... | collective-permute-start | bytes 3932168 | tf_op jit(solution)/shard_map/window/ppermute | solution.py:378
  98.0 1.3 copy-start.4
  131.1 7.7 %copy-start.10 = (s32[4,64]{1,0:T(4,128)S(1)}, s32[4,64]{1,0:T(4,128)}, u32[]{:S(2)}) copy-start(s32[4,64]{1,0:T(4,128)} %structure_ref.1) | copy-start | bytes 3076
  131.1 8.0 %copy-start.1 = (f32[4,256,256]{2,1,0:T(8,128)S(1)}, f32[4,256,256]{2,1,0:T(8,128)}, u32[]{:S(2)}) copy-start(f32[4,256,256]{2,1,0:T(8,128)} %t_ref.3) | copy-start | bytes 3145732
  132.1 17.6 %all-to-all-start.3 = ((f16[8,16,1152]{2,1,0:T(8,128)(2,1)}), f16[8,16,1152]{2,1,0:T(8,128)(2,1)}, u32[]{:S(2)}, u32[]{:S(2)}) async-start(f16[8,16,1152]{2,1,0:T(8,128)(2,1)} %broadcast_in_dim.10), calls=%async_computation.4 | async-start | bytes 589824 | tf_op jit(solution)/shard_map/window/all_to_all | solution.py:19
Sparse Core Ops, SparseCore 0:
  13.1 45.3 all-gather.1
  94.9 38.4 reduce-scatter.1

commit v4 on v3

--- a/solution.py
+++ b/solution.py
@@ -23,20 +23,35 @@
     return exchange(jnp.broadcast_to(x[None], (size,) + x.shape), axis)
 
 
-def local_call(kernel, shapes, scalars, *arrays, scratch=()):
+def local_call(kernel, shapes, scalars, *arrays, scratch=(), far=False, mebibytes=24):
     vmem = pl.BlockSpec(memory_space=pltpu.VMEM)
     smem = pl.BlockSpec(memory_space=pltpu.SMEM)
+    array_spec = pl.BlockSpec(memory_space=pl.ANY) if far else vmem
     return pl.pallas_call(
         kernel,
         out_shape=shapes,
-        in_specs=[smem] * len(scalars) + [vmem] * len(arrays),
+        in_specs=[smem] * len(scalars) + [array_spec] * len(arrays),
         out_specs=jax.tree.map(lambda _: vmem, shapes),
-        scratch_shapes=[pltpu.VMEM(*each) for each in scratch],
-        compiler_params=pltpu.CompilerParams(vmem_limit_bytes=24 * 1024 * 1024),
+        scratch_shapes=[
+            pltpu.VMEM(*each) if isinstance(each, tuple) else each for each in scratch
+        ],
+        compiler_params=pltpu.CompilerParams(vmem_limit_bytes=mebibytes * 1024 * 1024),
     )(*scalars, *arrays)
 
 
-def panel_kernel(structure_ref, place_ref, a_ref, w_ref, t_ref, message_ref, panel_ref):
+def panel_kernel(
+    place_ref, structure_far, a_far, w_far, t_far, message_ref, panel_ref,
+    structure_ref, a_ref, w_ref, t_ref, sems,
+):
+    pairs = [(structure_far, structure_ref), (a_far, a_ref), (w_far, w_ref)]
+    pairs += [(t_far.at[j], t_ref.at[j]) for j in range(t_ref.shape[0])]
+    copies = [
+        pltpu.make_async_copy(here, there, sems.at[i]) for i, (here, there) in enumerate(pairs)
+    ]
+    for copy in copies:
+        copy.start()
+    for copy in copies[:3]:
+        copy.wait()
     supernodes, width = t_ref.shape[0], t_ref.shape[1]
     local, wlocal = a_ref.shape[0], w_ref.shape[0]
     ha = supernodes * width // 2
@@ -46,6 +61,7 @@
     for j in range(supernodes):
         at = slice(j * width, (j + 1) * width)
         rows = jnp.concatenate([a_ref[:, at], w_ref[:, at]], axis=0)
+        copies[3 + j].wait()
         product = mm(rows, t_ref[j], HIGHEST)
         scale = structure_ref[j, place_ref[0]].astype(F32)
         a = (scale * product[:local]).astype(BF16)
@@ -159,7 +175,7 @@
 
 def window_kernel(
     core_ref, mine_ref, other_ref, high_ref, low_ref, lh_ref, ll_ref,
-    right_ref, keep_ref, send_ref, packed_ref, rh_ref, rl_ref, fh_ref, fl_ref,
+    right_ref, packed_ref, rh_ref, rl_ref, fh_ref, fl_ref,
 ):
     nc, nx, rows, _ = packed_ref.shape
     size, window = rh_ref.shape
@@ -198,8 +214,6 @@
                     row = ((k * nx + i) * nc + c) * rows
                     packed_ref[c, i, :, at : at + n] = part[row : row + rows]
             at += n
-    keep_ref[...] = packed_ref[core_ref[0]]
-    send_ref[...] = packed_ref[1 - core_ref[0]]
 
 
 def exponent(v):
@@ -207,10 +221,10 @@
     return jnp.floor(jnp.log2(jnp.maximum(top, 1e-30))) - 13.0
 
 
-def sum_kernel(a_ref, b_ref, out_ref):
-    nx, rows, n = a_ref.shape
+def sum_kernel(in_ref, out_ref):
+    _, nx, rows, n = in_ref.shape
     for i in range(nx):
-        total = a_ref[i] + b_ref[i]
+        total = in_ref[0, i] + in_ref[1, i]
         power = exponent(total)
         out_ref[i, :, :n] = total * jnp.exp2(-power)
         out_ref[i, :, n:] = jnp.broadcast_to(power, (rows, out_ref.shape[2] - n))
@@ -299,10 +313,20 @@
                 jax.ShapeDtypeStruct((nc, local + wlocal, ha), BF16),
                 jax.ShapeDtypeStruct((local, 2 * window), BF16),
             ),
-            (structure, place),
+            (place,),
+            structure,
             ancestor_rows,
             window_rows,
             tile_inverse,
+            scratch=(
+                pltpu.SMEM(structure.shape, jnp.int32),
+                (ancestor_rows.shape, F32),
+                (window_rows.shape, F32),
+                (tile_inverse.shape, F32),
+                pltpu.SemaphoreType.DMA((3 + supernodes,)),
+            ),
+            far=True,
+            mebibytes=56,
         )
 
     shape = lambda *dims, dtype=F32: jax.ShapeDtypeStruct(dims, dtype)
@@ -360,9 +384,9 @@
     with jax.named_scope("window"):
         half = ((ny * local, window), BF16)
         packed = (nx, wlocal, 2 * 10 * width)
-        right, keep, send = local_call(
+        right, packed_sum = local_call(
             window_kernel,
-            (shape(ny, local, window), shape(*packed), shape(*packed)),
+            (shape(ny, local, window), shape(nc, *packed)),
             (core,),
             own,
             away,
@@ -370,15 +394,15 @@
             low,
             lh,
             ll,
-            scratch=(((nc,) + packed, F32), half, half, half, half),
+            scratch=(half, half, half, half),
         )
         cross = lax.psum_scatter(right, "y", scatter_dimension=0, tiled=True)
         scale = jnp.repeat(select, width)[None, :]
         cross = -(scale * cross.reshape(local, window))
-        came = lax.ppermute(send, "c", swap)
+        packed_sum = exchange(packed_sum, "c").reshape(nc, *packed)
         half_type = jnp.float16
         n = packed[-1] + 128
-        parts = local_call(sum_kernel, shape(nx, wlocal, n), (), keep, came)
+        parts = local_call(sum_kernel, shape(nx, wlocal, n), (), packed_sum)
         parts = exchange(parts.astype(half_type), "x").astype(F32)
         spread = local_call(spread_kernel, shape(nz, wlocal, window + 128), (), parts)
         spread = exchange(spread.astype(half_type), "z").astype(F32)
@@ -396,6 +420,7 @@
             low,
             scratch=(spare, spare, ((width, window), F32)),
         )
+        base, cross = lax.optimization_barrier((base, cross))
         block = local_call(
             finish_kernel, shape(wlocal, window), (wtile.reshape(1),), spread, base
         )

time: 159 us -> 159 us (level)
  blocking collectives: 66.1 us -> 73.7 us
  local copies, waits for them, and re-layouts: 9.04 us -> 4.52 us
  waiting for transfers between devices: 24.6 us -> 22.8 us
    all_to_all x3 -> x4, blocking collectives: 33.5 us -> 41.3 us  [exchange(): return lax.all_to_all(x, axis, 0, 0, tiled=True)]
    unnamed x24 -> x16, local copies, waits for them, and re-layouts: 8.29 us -> 3.77 us
    ppermute x1 -> x0, waiting for transfers between devices: 3.19 us -> none  [body(): came = lax.ppermute(send, 'c', swap)]
    ppermute x1 -> x0, starting transfers between devices: 2.04 us -> none  [body(): came = lax.ppermute(send, 'c', swap)]
    all_to_all x1, waiting for transfers between devices: 5.81 us -> 7.42 us  [exchange(): return lax.all_to_all(x, axis, 0, 0, tiled=True)]
  transfers between devices with their start and end apart: 11 -> 10, of which waited for: 6 -> 5; matrix products, arithmetic and copies ran while one was open for 2% -> 1% of each run, Pallas kernels for 5% -> 4%
where the time goes in v4:
time: 159 us
  blocking collectives  73.7 us (46%)
  starting transfers between devices  26.1 us (16%)
  waiting for transfers between devices  22.8 us (14%)
  between operations  14.3 us (9%)
  Pallas kernels  13.6 us (9%)
  local copies, waits for them, and re-layouts  4.52 us (3%)
  other arithmetic  3.59 us (2%)
    all_to_all x4, blocking collectives, exchange(): return lax.all_to_all(x, axis, 0, 0, tiled=True)  41.3 us
    all_gather x1, blocking collectives, body(): got = lax.all_gather(got, 'z', axis=0, tiled=True)  32.5 us
    ppermute x3, waiting for transfers between devices, body(): lax.ppermute(first, 'x', [(i, (i + step) % nx) for i in range(nx)])  14.2 us
    pallas_call x12, Pallas kernels, local_call(): pl.pallas_call(kernel, out_shape=shapes, in_specs=[smem] * len(scalars) +...  13.6 us
    ppermute x3, starting transfers between devices, body(): lax.ppermute(first, 'x', [(i, (i + step) % nx) for i in range(nx)])  10.5 us
    all_to_all x1, starting transfers between devices, exchange(): return lax.all_to_all(x, axis, 0, 0, tiled=True)  7.9 us
    ppermute x4, starting transfers between devices, body(): others = [lax.ppermute(piece, 'c', swap) for piece in pieces]  7.65 us
    all_to_all x1, waiting for transfers between devices, exchange(): return lax.all_to_all(x, axis, 0, 0, tiled=True)  7.42 us
  transfers between devices with their start and end apart: 10, of which 5 were waited for; matrix products, arithmetic and copies ran while one was open for 1% of the time, Pallas kernels for 4%

profile of v4, /device:TPU:2, one launch (start us, length us, event | category | flops | bytes accessed | tf_op | source)
XLA Modules:
  0.0 158.7 jit_solution(13854722686647514666)
XLA Ops:
  7.2 0.0 all-gather.2.cloned.1.call-start
  7.3 0.6 pad_add_fusion.place_ref
  7.8 3.8 %panels.1 = (bf16[2,48,512]{2,1,0:T(8,128)(2,1)}, bf16[32,2048]{1,0:T(8,128)(2,1)}) custom-call(s32[3]{0:T(128)} %pad_add_fusion.place_ref, s32[4,64]{1,0:T(4,128)} %structure_far.1, f32[32,1024]{1,0:T(8,128)} %a_far.1, f32[16,1024]{1,0:T(8,128)} %w_far.1, f32[4,256,256]{2,1,0:T(8,128)} %t_ref.1), custom_call_target="tpu_custom_call" | custom-call | tf_op jit(solution)/shard_map/panels/pallas_call | solution.py:30
  11.7 0.0 copy-start.1
  11.7 0.0 all-gather.2.cloned.1.call-update
  11.7 0.0 reduce-scatter.2.cloned.1.call-start
  11.8 4.9 %all_to_all.25 = bf16[2,48,512]{2,1,0:T(8,128)(2,1)S(1)} all-to-all(bf16[2,48,512]{2,1,0:T(8,128)(2,1)} %get-tuple-element.12), channel_id=1, replica_groups=mesh['y'=8,'z'=8,'x'=4,'c'=2] {'c'}, dimensions={0} | all-to-all | bytes 196608 | tf_op jit(solution)/shard_map/gather/all_to_all | solution.py:19
  16.7 32.5 %all_gather.6.got_ref = bf16[16,48,512]{2,1,0:T(8,128)(2,1)S(1)} all-gather(bf16[2,48,512]{2,1,0:T(8,128)(2,1)S(1)} %all_to_all.25), channel_id=1, replica_groups=mesh['y'=8,'z'=8,'x'=4,'c'=2] {'z'}, dimensions={0}, use_global_device_ids=true | all-gather | bytes 884736 | tf_op jit(solution)/shard_map/gather/all_gather | solution.py:338
  49.2 3.4 %collective-permute-start = (bf16[608,512]{1,0:T(8,128)(2,1)S(1)}, bf16[608,512]{1,0:T(8,128)(2,1)S(1)}, u32[]{:S(2)}, u32[]{:S(2)}) collective-permute-start(bf16[608,512]{1,0:T(8,128)(2,1)S(1)} %gather.1.refs_0_.p0_ref), channel_id=1, source_target_pairs={{0,2},{2,4},{4,6},{6,0},{1,3},{3,5},{5,7},{7,1},{8,10},{10,12},{12... | collective-permute-start | bytes 1867784 | tf_op jit(solution)/shard_map/gather/ppermute | solution.py:346
  52.6 3.0 %collective-permute-start.1 = (bf16[608,512]{1,0:T(8,128)(2,1)S(1)}, bf16[608,512]{1,0:T(8,128)(2,1)S(1)}, u32[]{:S(2)}, u32[]{:S(2)}) collective-permute-start(bf16[608,512]{1,0:T(8,128)(2,1)S(1)} %gather.1.refs_0_.p0_ref), channel_id=1, source_target_pairs={{0,4},{2,6},{4,0},{6,2},{1,5},{3,7},{5,1},{7,3},{8,12},{10,14},{12... | collective-permute-start | bytes 1867784 | tf_op jit(solution)/shard_map/gather/ppermute | solution.py:346
  55.6 4.1 %collective-permute-start.2 = (bf16[608,512]{1,0:T(8,128)(2,1)S(1)}, bf16[608,512]{1,0:T(8,128)(2,1)S(1)}, u32[]{:S(2)}, u32[]{:S(2)}) collective-permute-start(bf16[608,512]{1,0:T(8,128)(2,1)S(1)} %gather.1.refs_0_.p0_ref), channel_id=1, source_target_pairs={{0,6},{2,0},{4,2},{6,4},{1,7},{3,1},{5,3},{7,5},{8,14},{10,8},{12,... | collective-permute-start | bytes 1867784 | tf_op jit(solution)/shard_map/gather/ppermute | solution.py:346
  59.7 1.9 %collective-permute-start.3 = (bf16[608,512]{1,0:T(8,128)(2,1)S(1)}, bf16[608,512]{1,0:T(8,128)(2,1)S(1)}, u32[]{:S(2)}, u32[]{:S(2)}) collective-permute-start(bf16[608,512]{1,0:T(8,128)(2,1)S(1)} %gather.1.refs_0_.p0_ref), channel_id=1, source_target_pairs={{0,1},{1,0},{2,3},{3,2},{4,5},{5,4},{6,7},{7,6},{8,9},{9,8},{10,11... | collective-permute-start | bytes 1867784 | tf_op jit(solution)/shard_map/gather/ppermute | solution.py:348
  61.6 6.4 %collective-permute-done.refs_1_.p1_ref = bf16[608,512]{1,0:T(8,128)(2,1)S(1)} collective-permute-done((bf16[608,512]{1,0:T(8,128)(2,1)S(1)}, bf16[608,512]{1,0:T(8,128)(2,1)S(1)}, u32[]{:S(2)}, u32[]{:S(2)}) %collective-permute-start) | collective-permute-done | bytes 622624 | tf_op jit(solution)/shard_map/gather/ppermute | solution.py:346
  68.0 1.9 %collective-permute-start.4 = (bf16[608,512]{1,0:T(8,128)(2,1)S(1)}, bf16[608,512]{1,0:T(8,128)(2,1)S(1)}, u32[]{:S(2)}, u32[]{:S(2)}) collective-permute-start(bf16[608,512]{1,0:T(8,128)(2,1)S(1)} %collective-permute-done.refs_1_.p1_ref), channel_id=1, source_target_pairs={{0,1},{1,0},{2,3},{3,2},{4,5},{5,4},{6,7},{7,6},{8,9},{9,8},{10,11... | collective-permute-start | bytes 1867784 | tf_op jit(solution)/shard_map/gather/ppermute | solution.py:348
  70.0 3.0 %collective-permute-done.1.refs_2_.p2_ref = bf16[608,512]{1,0:T(8,128)(2,1)S(1)} collective-permute-done((bf16[608,512]{1,0:T(8,128)(2,1)S(1)}, bf16[608,512]{1,0:T(8,128)(2,1)S(1)}, u32[]{:S(2)}, u32[]{:S(2)}) %collective-permute-start.1) | collective-permute-done | bytes 622624 | tf_op jit(solution)/shard_map/gather/ppermute | solution.py:346
  73.0 1.9 %collective-permute-start.5 = (bf16[608,512]{1,0:T(8,128)(2,1)S(1)}, bf16[608,512]{1,0:T(8,128)(2,1)S(1)}, u32[]{:S(2)}, u32[]{:S(2)}) collective-permute-start(bf16[608,512]{1,0:T(8,128)(2,1)S(1)} %collective-permute-done.1.refs_2_.p2_ref), channel_id=1, source_target_pairs={{0,1},{1,0},{2,3},{3,2},{4,5},{5,4},{6,7},{7,6},{8,9},{9,8},{10,11... | collective-permute-start | bytes 1867784 | tf_op jit(solution)/shard_map/gather/ppermute | solution.py:348
  74.9 4.8 %collective-permute-done.2.refs_3_.p3_ref = bf16[608,512]{1,0:T(8,128)(2,1)S(1)} collective-permute-done((bf16[608,512]{1,0:T(8,128)(2,1)S(1)}, bf16[608,512]{1,0:T(8,128)(2,1)S(1)}, u32[]{:S(2)}, u32[]{:S(2)}) %collective-permute-start.2) | collective-permute-done | bytes 622624 | tf_op jit(solution)/shard_map/gather/ppermute | solution.py:346
  79.6 1.9 %collective-permute-start.6 = (bf16[608,512]{1,0:T(8,128)(2,1)S(1)}, bf16[608,512]{1,0:T(8,128)(2,1)S(1)}, u32[]{:S(2)}, u32[]{:S(2)}) collective-permute-start(bf16[608,512]{1,0:T(8,128)(2,1)S(1)} %collective-permute-done.2.refs_3_.p3_ref), channel_id=1, source_target_pairs={{0,1},{1,0},{2,3},{3,2},{4,5},{5,4},{6,7},{7,6},{8,9},{9,8},{10,11... | collective-permute-start | bytes 1867784 | tf_op jit(solution)/shard_map/gather/ppermute | solution.py:348
  81.6 0.8 product.2.mine_ref
  82.4 0.0 collective-permute-done.3.refs_4_.p0_ref
  82.4 1.1 collective-permute-done.6.refs_7_.p3_ref
  83.6 0.8 product.3.other_ref
  84.4 0.5 unit_inverse.2
  84.9 0.0 all-gather.2.cloned.1.call-done.panel_ref
  84.9 1.2 copy-done.3
  86.1 0.6 unit_inverse.3
  86.8 2.1 %window.4 = (f32[8,32,1024]{2,1,0:T(8,128)S(1)}, f32[2,4,16,5120]{3,2,1,0:T(8,128)S(1)}) custom-call(s32[1]{0:T(128)} %bitcast.3.core_ref, f32[256,512]{1,0:T(8,128)S(1)} %product.2.mine_ref, f32[256,512]{1,0:T(8,128)S(1)} %product.3.other_ref, bf16[768,768]{1,0:T(8,128)(2,1)S(1)} %get-tuple-element.13.high_ref, ...), custom_call_target="tpu_custom_call" | custom-call | tf_op jit(solution)/shard_map/window/pallas_call | solution.py:30
  88.9 1.5 copy-done.2
  90.4 1.0 copy-done.4
  91.4 0.0 reduce-scatter.2.cloned.1.call-update
  91.4 7.1 %all_to_all.26.in_ref = f32[2,4,16,5120]{3,2,1,0:T(8,128)S(1)} all-to-all(f32[2,4,16,5120]{3,2,1,0:T(8,128)} %copy-done.2), channel_id=1, replica_groups=mesh['y'=8,'z'=8,'x'=4,'c'=2] {'c'}, dimensions={0} | all-to-all | bytes 5242880 | tf_op jit(solution)/shard_map/window/all_to_all | solution.py:19
  98.5 0.4 window.5
  98.8 0.1 convert_element_type.26
  98.9 13.6 %all_to_all.27 = f16[4,16,5248]{2,1,0:T(8,128)(2,1)S(1)} all-to-all(f16[4,16,5248]{2,1,0:T(8,128)(2,1)S(1)} %convert_element_type.26), channel_id=1, replica_groups=mesh['y'=8,'z'=8,'x'=4,'c'=2] {'x'}, dimensions={0} | all-to-all | bytes 1343488 | tf_op jit(solution)/shard_map/window/all_to_all | solution.py:19
  112.6 0.1 convert_element_type.27.in_ref
  112.7 0.3 window.6
  113.0 15.6 %all_to_all.28 = f16[8,16,1152]{2,1,0:T(8,128)(2,1)S(1)} all-to-all(f16[8,16,1152]{2,1,0:T(8,128)(2,1)S(1)} %convert_element_type.28), channel_id=1, replica_groups=mesh['y'=8,'z'=8,'x'=4,'c'=2] {'z'}, dimensions={0} | all-to-all | bytes 589824 | tf_op jit(solution)/shard_map/window/all_to_all | solution.py:19
  128.7 0.2 window.7
  128.9 0.7 broadcast_in_dim.10
  129.7 7.9 %all-to-all-start.4 = ((f16[8,16,1152]{2,1,0:T(8,128)(2,1)}), f16[8,16,1152]{2,1,0:T(8,128)(2,1)}, u32[]{:S(2)}, u32[]{:S(2)}) async-start(f16[8,16,1152]{2,1,0:T(8,128)(2,1)} %broadcast_in_dim.10), calls=%async_computation.5 | async-start | bytes 589824 | tf_op jit(solution)/shard_map/window/all_to_all | solution.py:19
  137.6 0.2 convert_reduce_fusion
  137.8 0.1 broadcast_bitcast_fusion
  137.9 3.2 %diagonal.2.base_ref = f32[16,1024]{1,0:T(8,128)S(1)} custom-call(s32[3]{0:T(128)S(1)} %copy-done.5, f32[4,256,256]{2,1,0:T(8,128)S(1)} %copy-done, bf16[768,768]{1,0:T(8,128)(2,1)S(1)} %get-tuple-element.13.high_ref, bf16[768,768]{1,0:T(8,128)(2,1)S(1)} %get-tuple-element.14.low_ref), custom_call_target="tpu_custom_call" | custom-call | tf_op jit(solution)/shard_map/diagonal/pallas_call | solution.py:30
  141.1 7.4 %all-to-all-done.4 = f16[8,16,1152]{2,1,0:T(8,128)(2,1)} async-done(((f16[8,16,1152]{2,1,0:T(8,128)(2,1)}), f16[8,16,1152]{2,1,0:T(8,128)(2,1)}, u32[]{:S(2)}, u32[]{:S(2)}) %all-to-all-start.4) | async-done | bytes 294944 | tf_op jit(solution)/shard_map/window/all_to_all | solution.py:19
  148.5 1.0 convert_element_type.31.in_ref
  149.5 0.0 reduce-scatter.2.cloned.1.call-done
  149.6 1.6 fusion
  151.1 0.7 diagonal.3
  (17 shorter events, 0.2 us)
Async XLA Ops:
  7.2 77.8 %all-gather.2.cloned.1.call-start = ((), (), s32[]{:S(2)}) async-start(), calls=%async_computation.6 | async-start | bytes 1179648 | tf_op jit(solution)/shard_map/column_block/all_gather | solution.py:334
  11.7 69.9 %copy-start.1 = (bf16[2048,8,1,32]{0,3,2,1:T(8,128)(2,1)S(1)}, bf16[2048,8,1,32]{0,3,2,1:T(8,128)(2,1)}, u32[]{:S(2)}) copy-start(bf16[2048,8,1,32]{0,3,2,1:T(8,128)(2,1)} %param.5) | copy-start | bytes 3145732
  11.7 137.8 %reduce-scatter.2.cloned.1.call-start = ((), (), s32[]{:S(2)}) async-start(), calls=%async_computation.7 | async-start | bytes 1179648 | tf_op jit(solution)/shard_map/window/reduce_scatter | solution.py:399
  49.2 18.9 %collective-permute-start = (bf16[608,512]{1,0:T(8,128)(2,1)S(1)}, bf16[608,512]{1,0:T(8,128)(2,1)S(1)}, u32[]{:S(2)}, u32[]{:S(2)}) collective-permute-start(bf16[608,512]{1,0:T(8,128)(2,1)S(1)} %gather.1.refs_0_.p0_ref), channel_id=1, source_target_pairs={{0,2},{2,4},{4,6},{6,0},{1,3},{3,5},{5,7},{7,1},{8,10},{10,12},{12... | collective-permute-start | bytes 1867784 | tf_op jit(solution)/shard_map/gather/ppermute | solution.py:346
  52.6 20.4 %collective-permute-start.1 = (bf16[608,512]{1,0:T(8,128)(2,1)S(1)}, bf16[608,512]{1,0:T(8,128)(2,1)S(1)}, u32[]{:S(2)}, u32[]{:S(2)}) collective-permute-start(bf16[608,512]{1,0:T(8,128)(2,1)S(1)} %gather.1.refs_0_.p0_ref), channel_id=1, source_target_pairs={{0,4},{2,6},{4,0},{6,2},{1,5},{3,7},{5,1},{7,3},{8,12},{10,14},{12... | collective-permute-start | bytes 1867784 | tf_op jit(solution)/shard_map/gather/ppermute | solution.py:346
  55.6 24.0 %collective-permute-start.2 = (bf16[608,512]{1,0:T(8,128)(2,1)S(1)}, bf16[608,512]{1,0:T(8,128)(2,1)S(1)}, u32[]{:S(2)}, u32[]{:S(2)}) collective-permute-start(bf16[608,512]{1,0:T(8,128)(2,1)S(1)} %gather.1.refs_0_.p0_ref), channel_id=1, source_target_pairs={{0,6},{2,0},{4,2},{6,4},{1,7},{3,1},{5,3},{7,5},{8,14},{10,8},{12,... | collective-permute-start | bytes 1867784 | tf_op jit(solution)/shard_map/gather/ppermute | solution.py:346
  59.7 22.7 %collective-permute-start.3 = (bf16[608,512]{1,0:T(8,128)(2,1)S(1)}, bf16[608,512]{1,0:T(8,128)(2,1)S(1)}, u32[]{:S(2)}, u32[]{:S(2)}) collective-permute-start(bf16[608,512]{1,0:T(8,128)(2,1)S(1)} %gather.1.refs_0_.p0_ref), channel_id=1, source_target_pairs={{0,1},{1,0},{2,3},{3,2},{4,5},{5,4},{6,7},{7,6},{8,9},{9,8},{10,11... | collective-permute-start | bytes 1867784 | tf_op jit(solution)/shard_map/gather/ppermute | solution.py:348
  68.0 14.4 %collective-permute-start.4 = (bf16[608,512]{1,0:T(8,128)(2,1)S(1)}, bf16[608,512]{1,0:T(8,128)(2,1)S(1)}, u32[]{:S(2)}, u32[]{:S(2)}) collective-permute-start(bf16[608,512]{1,0:T(8,128)(2,1)S(1)} %collective-permute-done.refs_1_.p1_ref), channel_id=1, source_target_pairs={{0,1},{1,0},{2,3},{3,2},{4,5},{5,4},{6,7},{7,6},{8,9},{9,8},{10,11... | collective-permute-start | bytes 1867784 | tf_op jit(solution)/shard_map/gather/ppermute | solution.py:348
  73.0 9.5 %collective-permute-start.5 = (bf16[608,512]{1,0:T(8,128)(2,1)S(1)}, bf16[608,512]{1,0:T(8,128)(2,1)S(1)}, u32[]{:S(2)}, u32[]{:S(2)}) collective-permute-start(bf16[608,512]{1,0:T(8,128)(2,1)S(1)} %collective-permute-done.1.refs_2_.p2_ref), channel_id=1, source_target_pairs={{0,1},{1,0},{2,3},{3,2},{4,5},{5,4},{6,7},{7,6},{8,9},{9,8},{10,11... | collective-permute-start | bytes 1867784 | tf_op jit(solution)/shard_map/gather/ppermute | solution.py:348
  79.6 3.9 %collective-permute-start.6 = (bf16[608,512]{1,0:T(8,128)(2,1)S(1)}, bf16[608,512]{1,0:T(8,128)(2,1)S(1)}, u32[]{:S(2)}, u32[]{:S(2)}) collective-permute-start(bf16[608,512]{1,0:T(8,128)(2,1)S(1)} %collective-permute-done.2.refs_3_.p3_ref), channel_id=1, source_target_pairs={{0,1},{1,0},{2,3},{3,2},{4,5},{5,4},{6,7},{7,6},{8,9},{9,8},{10,11... | collective-permute-start | bytes 1867784 | tf_op jit(solution)/shard_map/gather/ppermute | solution.py:348
  84.9 1.2 copy-start.3
  88.9 1.5 copy-start.2
  90.4 1.0 copy-start.4
  128.6 9.0 %copy-start.6 = (s32[4,64]{1,0:T(4,128)S(1)}, s32[4,64]{1,0:T(4,128)}, u32[]{:S(2)}) copy-start(s32[4,64]{1,0:T(4,128)} %structure_far.1) | copy-start | bytes 3076
  128.6 9.2 %copy-start = (f32[4,256,256]{2,1,0:T(8,128)S(1)}, f32[4,256,256]{2,1,0:T(8,128)}, u32[]{:S(2)}) copy-start(f32[4,256,256]{2,1,0:T(8,128)} %t_ref.1) | copy-start | bytes 3145732
  128.6 9.2 %copy-start.5 = (s32[3]{0:T(128)S(1)}, s32[3]{0:T(128)}, u32[]{:S(2)}) copy-start(s32[3]{0:T(128)} %pad_add_fusion.place_ref) | copy-start | bytes 40
  129.7 18.8 %all-to-all-start.4 = ((f16[8,16,1152]{2,1,0:T(8,128)(2,1)}), f16[8,16,1152]{2,1,0:T(8,128)(2,1)}, u32[]{:S(2)}, u32[]{:S(2)}) async-start(f16[8,16,1152]{2,1,0:T(8,128)(2,1)} %broadcast_in_dim.10), calls=%async_computation.5 | async-start | bytes 589824 | tf_op jit(solution)/shard_map/window/all_to_all | solution.py:19
Sparse Core Ops, SparseCore 0:
  11.8 45.4 all-gather.1
  91.5 39.2 reduce-scatter.1

commit v5 on v4

--- a/solution.py
+++ b/solution.py
@@ -174,7 +174,7 @@
 
 
 def window_kernel(
-    core_ref, mine_ref, other_ref, high_ref, low_ref, lh_ref, ll_ref,
+    core_ref, structure_ref, z_ref, mine_ref, other_ref, high_ref, low_ref, lh_ref, ll_ref,
     right_ref, packed_ref, rh_ref, rl_ref, fh_ref, fl_ref,
 ):
     nc, nx, rows, _ = packed_ref.shape
@@ -199,7 +199,8 @@
             )
         cut = slice(j * width, (j + 1) * width)
         for i in range(ny):
-            right_ref[i, :, cut] = value[i * local : (i + 1) * local]
+            select = structure_ref[j, i * ny + z_ref[0]].astype(F32)
+            right_ref[i, :, cut] = -(select * value[i * local : (i + 1) * local])
         rh_ref[:, cut], rl_ref[:, cut] = split(value)
     at = 0
     for t in range(4):
@@ -302,7 +303,6 @@
     col = (z * nx + x) * nc + c
     tile = ((y * (nz * nx * nc) + col) * local) // width
     wtile = (col * wlocal) // width
-    select = lax.dynamic_slice_in_dim(structure, tile, 1, 1)[:, 0].astype(F32)
 
     with jax.named_scope("panels"):
         ha, hw = window // 2, (window - width) // 2
@@ -387,7 +387,7 @@
         right, packed_sum = local_call(
             window_kernel,
             (shape(ny, local, window), shape(nc, *packed)),
-            (core,),
+            (core, structure, z.reshape(1)),
             own,
             away,
             high,
@@ -397,8 +397,7 @@
             scratch=(half, half, half, half),
         )
         cross = lax.psum_scatter(right, "y", scatter_dimension=0, tiled=True)
-        scale = jnp.repeat(select, width)[None, :]
-        cross = -(scale * cross.reshape(local, window))
+        cross = cross.reshape(local, window)
         packed_sum = exchange(packed_sum, "c").reshape(nc, *packed)
         half_type = jnp.float16
         n = packed[-1] + 128
@@ -420,7 +419,6 @@
             low,
             scratch=(spare, spare, ((width, window), F32)),
         )
-        base, cross = lax.optimization_barrier((base, cross))
         block = local_call(
             finish_kernel, shape(wlocal, window), (wtile.reshape(1),), spread, base
         )

time: 159 us -> 159 us (level)
  other arithmetic: 3.59 us -> 1.86 us
    unnamed x16 -> x14, local copies, waits for them, and re-layouts: 3.77 us -> 3.73 us
where the time goes in v5:
time: 159 us; the launch traced here: 158 us
  blocking collectives  73.7 us (46%)
  starting transfers between devices  26.1 us (16%)
  waiting for transfers between devices  23.1 us (15%)
  between operations  14.3 us (9%)
  Pallas kernels  14.2 us (9%)
  local copies, waits for them, and re-layouts  4.47 us (3%)
  other arithmetic  1.86 us (1%)
    all_to_all x4, blocking collectives, exchange(): return lax.all_to_all(x, axis, 0, 0, tiled=True)  41.3 us
    all_gather x1, blocking collectives, body(): got = lax.all_gather(got, 'z', axis=0, tiled=True)  32.5 us
    ppermute x3, waiting for transfers between devices, body(): lax.ppermute(first, 'x', [(i, (i + step) % nx) for i in range(nx)])  14.2 us
    pallas_call x12, Pallas kernels, local_call(): pl.pallas_call(kernel, out_shape=shapes, in_specs=[smem] * len(scalars) +...  14.2 us
    ppermute x3, starting transfers between devices, body(): lax.ppermute(first, 'x', [(i, (i + step) % nx) for i in range(nx)])  10.5 us
    all_to_all x1, starting transfers between devices, exchange(): return lax.all_to_all(x, axis, 0, 0, tiled=True)  7.9 us
    all_to_all x1, waiting for transfers between devices, exchange(): return lax.all_to_all(x, axis, 0, 0, tiled=True)  7.69 us
    ppermute x4, starting transfers between devices, body(): others = [lax.ppermute(piece, 'c', swap) for piece in pieces]  7.65 us
  transfers between devices with their start and end apart: 10, of which 5 were waited for; matrix products, arithmetic and copies ran while one was open for 1% of the time, Pallas kernels for 4%

profile of v5, /device:TPU:2, one launch (start us, length us, event | category | flops | bytes accessed | tf_op | source)
XLA Modules:
  0.0 157.7 jit_solution(15265856267378217980)
XLA Ops:
  7.2 0.0 all-gather.2.cloned.1.call-start
  7.3 0.6 pad_add_fusion.place_ref
  7.9 3.8 %panels.1 = (bf16[2,48,512]{2,1,0:T(8,128)(2,1)}, bf16[32,2048]{1,0:T(8,128)(2,1)}) custom-call(s32[3]{0:T(128)} %pad_add_fusion.place_ref, s32[4,64]{1,0:T(4,128)} %structure_ref.1, f32[32,1024]{1,0:T(8,128)} %a_far.1, f32[16,1024]{1,0:T(8,128)} %w_far.1, f32[4,256,256]{2,1,0:T(8,128)} %t_ref.1), custom_call_target="tpu_custom_call" | custom-call | tf_op jit(solution)/shard_map/panels/pallas_call | solution.py:30
  11.7 0.0 copy-start.1
  11.7 0.0 all-gather.2.cloned.1.call-update
  11.7 0.0 reduce-scatter.2.cloned.1.call-start
  11.8 4.9 %all_to_all.25 = bf16[2,48,512]{2,1,0:T(8,128)(2,1)S(1)} all-to-all(bf16[2,48,512]{2,1,0:T(8,128)(2,1)} %get-tuple-element.10), channel_id=1, replica_groups=mesh['y'=8,'z'=8,'x'=4,'c'=2] {'c'}, dimensions={0} | all-to-all | bytes 196608 | tf_op jit(solution)/shard_map/gather/all_to_all | solution.py:19
  16.7 32.5 %all_gather.6.got_ref = bf16[16,48,512]{2,1,0:T(8,128)(2,1)S(1)} all-gather(bf16[2,48,512]{2,1,0:T(8,128)(2,1)S(1)} %all_to_all.25), channel_id=1, replica_groups=mesh['y'=8,'z'=8,'x'=4,'c'=2] {'z'}, dimensions={0}, use_global_device_ids=true | all-gather | bytes 884736 | tf_op jit(solution)/shard_map/gather/all_gather | solution.py:338
  49.2 3.4 %collective-permute-start = (bf16[608,512]{1,0:T(8,128)(2,1)S(1)}, bf16[608,512]{1,0:T(8,128)(2,1)S(1)}, u32[]{:S(2)}, u32[]{:S(2)}) collective-permute-start(bf16[608,512]{1,0:T(8,128)(2,1)S(1)} %gather.1.p0_ref.refs_0_), channel_id=1, source_target_pairs={{0,2},{2,4},{4,6},{6,0},{1,3},{3,5},{5,7},{7,1},{8,10},{10,12},{12... | collective-permute-start | bytes 1867784 | tf_op jit(solution)/shard_map/gather/ppermute | solution.py:346
  52.6 3.0 %collective-permute-start.1 = (bf16[608,512]{1,0:T(8,128)(2,1)S(1)}, bf16[608,512]{1,0:T(8,128)(2,1)S(1)}, u32[]{:S(2)}, u32[]{:S(2)}) collective-permute-start(bf16[608,512]{1,0:T(8,128)(2,1)S(1)} %gather.1.p0_ref.refs_0_), channel_id=1, source_target_pairs={{0,4},{2,6},{4,0},{6,2},{1,5},{3,7},{5,1},{7,3},{8,12},{10,14},{12... | collective-permute-start | bytes 1867784 | tf_op jit(solution)/shard_map/gather/ppermute | solution.py:346
  55.6 4.1 %collective-permute-start.2 = (bf16[608,512]{1,0:T(8,128)(2,1)S(1)}, bf16[608,512]{1,0:T(8,128)(2,1)S(1)}, u32[]{:S(2)}, u32[]{:S(2)}) collective-permute-start(bf16[608,512]{1,0:T(8,128)(2,1)S(1)} %gather.1.p0_ref.refs_0_), channel_id=1, source_target_pairs={{0,6},{2,0},{4,2},{6,4},{1,7},{3,1},{5,3},{7,5},{8,14},{10,8},{12,... | collective-permute-start | bytes 1867784 | tf_op jit(solution)/shard_map/gather/ppermute | solution.py:346
  59.7 1.9 %collective-permute-start.3 = (bf16[608,512]{1,0:T(8,128)(2,1)S(1)}, bf16[608,512]{1,0:T(8,128)(2,1)S(1)}, u32[]{:S(2)}, u32[]{:S(2)}) collective-permute-start(bf16[608,512]{1,0:T(8,128)(2,1)S(1)} %gather.1.p0_ref.refs_0_), channel_id=1, source_target_pairs={{0,1},{1,0},{2,3},{3,2},{4,5},{5,4},{6,7},{7,6},{8,9},{9,8},{10,11... | collective-permute-start | bytes 1867784 | tf_op jit(solution)/shard_map/gather/ppermute | solution.py:348
  61.6 6.4 %collective-permute-done.p1_ref.refs_1_ = bf16[608,512]{1,0:T(8,128)(2,1)S(1)} collective-permute-done((bf16[608,512]{1,0:T(8,128)(2,1)S(1)}, bf16[608,512]{1,0:T(8,128)(2,1)S(1)}, u32[]{:S(2)}, u32[]{:S(2)}) %collective-permute-start) | collective-permute-done | bytes 622624 | tf_op jit(solution)/shard_map/gather/ppermute | solution.py:346
  68.1 1.9 %collective-permute-start.4 = (bf16[608,512]{1,0:T(8,128)(2,1)S(1)}, bf16[608,512]{1,0:T(8,128)(2,1)S(1)}, u32[]{:S(2)}, u32[]{:S(2)}) collective-permute-start(bf16[608,512]{1,0:T(8,128)(2,1)S(1)} %collective-permute-done.p1_ref.refs_1_), channel_id=1, source_target_pairs={{0,1},{1,0},{2,3},{3,2},{4,5},{5,4},{6,7},{7,6},{8,9},{9,8},{10,11... | collective-permute-start | bytes 1867784 | tf_op jit(solution)/shard_map/gather/ppermute | solution.py:348
  70.0 3.0 %collective-permute-done.1.p2_ref.refs_2_ = bf16[608,512]{1,0:T(8,128)(2,1)S(1)} collective-permute-done((bf16[608,512]{1,0:T(8,128)(2,1)S(1)}, bf16[608,512]{1,0:T(8,128)(2,1)S(1)}, u32[]{:S(2)}, u32[]{:S(2)}) %collective-permute-start.1) | collective-permute-done | bytes 622624 | tf_op jit(solution)/shard_map/gather/ppermute | solution.py:346
  73.0 1.9 %collective-permute-start.5 = (bf16[608,512]{1,0:T(8,128)(2,1)S(1)}, bf16[608,512]{1,0:T(8,128)(2,1)S(1)}, u32[]{:S(2)}, u32[]{:S(2)}) collective-permute-start(bf16[608,512]{1,0:T(8,128)(2,1)S(1)} %collective-permute-done.1.p2_ref.refs_2_), channel_id=1, source_target_pairs={{0,1},{1,0},{2,3},{3,2},{4,5},{5,4},{6,7},{7,6},{8,9},{9,8},{10,11... | collective-permute-start | bytes 1867784 | tf_op jit(solution)/shard_map/gather/ppermute | solution.py:348
  74.9 4.8 %collective-permute-done.2.p3_ref.refs_3_ = bf16[608,512]{1,0:T(8,128)(2,1)S(1)} collective-permute-done((bf16[608,512]{1,0:T(8,128)(2,1)S(1)}, bf16[608,512]{1,0:T(8,128)(2,1)S(1)}, u32[]{:S(2)}, u32[]{:S(2)}) %collective-permute-start.2) | collective-permute-done | bytes 622624 | tf_op jit(solution)/shard_map/gather/ppermute | solution.py:346
  79.7 1.9 %collective-permute-start.6 = (bf16[608,512]{1,0:T(8,128)(2,1)S(1)}, bf16[608,512]{1,0:T(8,128)(2,1)S(1)}, u32[]{:S(2)}, u32[]{:S(2)}) collective-permute-start(bf16[608,512]{1,0:T(8,128)(2,1)S(1)} %collective-permute-done.2.p3_ref.refs_3_), channel_id=1, source_target_pairs={{0,1},{1,0},{2,3},{3,2},{4,5},{5,4},{6,7},{7,6},{8,9},{9,8},{10,11... | collective-permute-start | bytes 1867784 | tf_op jit(solution)/shard_map/gather/ppermute | solution.py:348
  81.6 0.8 product.2.mine_ref
  82.4 0.0 collective-permute-done.3.p0_ref.refs_4_
  82.4 0.0 collective-permute-done.4.p1_ref.refs_5_
  82.5 0.0 collective-permute-done.5.p2_ref.refs_6_
  82.5 1.1 collective-permute-done.6.p3_ref.refs_7_
  83.6 0.8 product.3.other_ref
  84.4 0.5 unit_inverse.2
  84.9 0.0 all-gather.2.cloned.1.call-done.panel_ref
  84.9 1.2 copy-done.3
  86.2 0.6 unit_inverse.3
  86.8 0.0 copy-done.5
  86.8 2.7 %window.4 = (f32[8,32,1024]{2,1,0:T(8,128)S(1)}, f32[2,4,16,5120]{3,2,1,0:T(8,128)S(1)}) custom-call(s32[1]{0:T(128)} %bitcast.core_ref, s32[4,64]{1,0:T(4,128)S(1)} %copy-done.5, s32[1]{0:T(128)} %bitcast.1.z_ref, f32[256,512]{1,0:T(8,128)S(1)} %product.2.mine_ref, f32[256,512]{1,0:T(8,128)S(1)} %product.3.other_ref, ...), custom_call_target="tpu_custom_call" | custom-call | tf_op jit(solution)/shard_map/window/pallas_call | solution.py:30
  89.6 1.5 copy-done.2
  91.0 1.0 copy-done.4
  92.0 0.0 reduce-scatter.2.cloned.1.call-update
  92.0 7.1 %all_to_all.26.in_ref = f32[2,4,16,5120]{3,2,1,0:T(8,128)S(1)} all-to-all(f32[2,4,16,5120]{3,2,1,0:T(8,128)} %copy-done.2), channel_id=1, replica_groups=mesh['y'=8,'z'=8,'x'=4,'c'=2] {'c'}, dimensions={0} | all-to-all | bytes 5242880 | tf_op jit(solution)/shard_map/window/all_to_all | solution.py:19
  99.1 0.4 window.5
  99.5 0.1 convert_element_type.18
  99.6 13.6 %all_to_all.27 = f16[4,16,5248]{2,1,0:T(8,128)(2,1)S(1)} all-to-all(f16[4,16,5248]{2,1,0:T(8,128)(2,1)S(1)} %convert_element_type.18), channel_id=1, replica_groups=mesh['y'=8,'z'=8,'x'=4,'c'=2] {'x'}, dimensions={0} | all-to-all | bytes 1343488 | tf_op jit(solution)/shard_map/window/all_to_all | solution.py:19
  113.2 0.1 convert_element_type.19.in_ref
  113.3 0.3 window.6
  113.7 15.6 %all_to_all.28 = f16[8,16,1152]{2,1,0:T(8,128)(2,1)S(1)} all-to-all(f16[8,16,1152]{2,1,0:T(8,128)(2,1)S(1)} %convert_element_type.20), channel_id=1, replica_groups=mesh['y'=8,'z'=8,'x'=4,'c'=2] {'z'}, dimensions={0} | all-to-all | bytes 589824 | tf_op jit(solution)/shard_map/window/all_to_all | solution.py:19
  129.3 0.2 window.7
  129.6 0.7 broadcast_in_dim.2
  130.3 7.9 %all-to-all-start.4 = ((f16[8,16,1152]{2,1,0:T(8,128)(2,1)}), f16[8,16,1152]{2,1,0:T(8,128)(2,1)}, u32[]{:S(2)}, u32[]{:S(2)}) async-start(f16[8,16,1152]{2,1,0:T(8,128)(2,1)} %broadcast_in_dim.2), calls=%async_computation.5 | async-start | bytes 589824 | tf_op jit(solution)/shard_map/window/all_to_all | solution.py:19
  138.2 0.0 copy-done
  138.2 3.2 %diagonal.2.base_ref = f32[16,1024]{1,0:T(8,128)S(1)} custom-call(s32[3]{0:T(128)S(1)} %copy-done.6, f32[4,256,256]{2,1,0:T(8,128)S(1)} %copy-done, bf16[768,768]{1,0:T(8,128)(2,1)S(1)} %get-tuple-element.11.high_ref, bf16[768,768]{1,0:T(8,128)(2,1)S(1)} %get-tuple-element.12.low_ref), custom_call_target="tpu_custom_call" | custom-call | tf_op jit(solution)/shard_map/diagonal/pallas_call | solution.py:30
  141.5 7.7 %all-to-all-done.4 = f16[8,16,1152]{2,1,0:T(8,128)(2,1)} async-done(((f16[8,16,1152]{2,1,0:T(8,128)(2,1)}), f16[8,16,1152]{2,1,0:T(8,128)(2,1)}, u32[]{:S(2)}, u32[]{:S(2)}) %all-to-all-start.4) | async-done | bytes 294944 | tf_op jit(solution)/shard_map/window/all_to_all | solution.py:19
  149.2 1.0 convert_element_type.23.in_ref
  150.2 0.7 diagonal.3
  (13 shorter events, 0.1 us)
Async XLA Ops:
  7.2 77.8 %all-gather.2.cloned.1.call-start = ((), (), s32[]{:S(2)}) async-start(), calls=%async_computation.6 | async-start | bytes 1179648 | tf_op jit(solution)/shard_map/column_block/all_gather | solution.py:334
  11.7 69.9 %copy-start.1 = (bf16[2048,8,1,32]{0,3,2,1:T(8,128)(2,1)S(1)}, bf16[2048,8,1,32]{0,3,2,1:T(8,128)(2,1)}, u32[]{:S(2)}) copy-start(bf16[2048,8,1,32]{0,3,2,1:T(8,128)(2,1)} %param.5) | copy-start | bytes 3145732
  11.7 139.2 %reduce-scatter.2.cloned.1.call-start = ((), (), s32[]{:S(2)}) async-start(), calls=%async_computation.7 | async-start | bytes 1179648 | tf_op jit(solution)/shard_map/window/reduce_scatter | solution.py:399
  49.2 18.9 %collective-permute-start = (bf16[608,512]{1,0:T(8,128)(2,1)S(1)}, bf16[608,512]{1,0:T(8,128)(2,1)S(1)}, u32[]{:S(2)}, u32[]{:S(2)}) collective-permute-start(bf16[608,512]{1,0:T(8,128)(2,1)S(1)} %gather.1.p0_ref.refs_0_), channel_id=1, source_target_pairs={{0,2},{2,4},{4,6},{6,0},{1,3},{3,5},{5,7},{7,1},{8,10},{10,12},{12... | collective-permute-start | bytes 1867784 | tf_op jit(solution)/shard_map/gather/ppermute | solution.py:346
  52.6 20.4 %collective-permute-start.1 = (bf16[608,512]{1,0:T(8,128)(2,1)S(1)}, bf16[608,512]{1,0:T(8,128)(2,1)S(1)}, u32[]{:S(2)}, u32[]{:S(2)}) collective-permute-start(bf16[608,512]{1,0:T(8,128)(2,1)S(1)} %gather.1.p0_ref.refs_0_), channel_id=1, source_target_pairs={{0,4},{2,6},{4,0},{6,2},{1,5},{3,7},{5,1},{7,3},{8,12},{10,14},{12... | collective-permute-start | bytes 1867784 | tf_op jit(solution)/shard_map/gather/ppermute | solution.py:346
  55.6 24.0 %collective-permute-start.2 = (bf16[608,512]{1,0:T(8,128)(2,1)S(1)}, bf16[608,512]{1,0:T(8,128)(2,1)S(1)}, u32[]{:S(2)}, u32[]{:S(2)}) collective-permute-start(bf16[608,512]{1,0:T(8,128)(2,1)S(1)} %gather.1.p0_ref.refs_0_), channel_id=1, source_target_pairs={{0,6},{2,0},{4,2},{6,4},{1,7},{3,1},{5,3},{7,5},{8,14},{10,8},{12,... | collective-permute-start | bytes 1867784 | tf_op jit(solution)/shard_map/gather/ppermute | solution.py:346
  59.7 22.7 %collective-permute-start.3 = (bf16[608,512]{1,0:T(8,128)(2,1)S(1)}, bf16[608,512]{1,0:T(8,128)(2,1)S(1)}, u32[]{:S(2)}, u32[]{:S(2)}) collective-permute-start(bf16[608,512]{1,0:T(8,128)(2,1)S(1)} %gather.1.p0_ref.refs_0_), channel_id=1, source_target_pairs={{0,1},{1,0},{2,3},{3,2},{4,5},{5,4},{6,7},{7,6},{8,9},{9,8},{10,11... | collective-permute-start | bytes 1867784 | tf_op jit(solution)/shard_map/gather/ppermute | solution.py:348
  68.1 14.4 %collective-permute-start.4 = (bf16[608,512]{1,0:T(8,128)(2,1)S(1)}, bf16[608,512]{1,0:T(8,128)(2,1)S(1)}, u32[]{:S(2)}, u32[]{:S(2)}) collective-permute-start(bf16[608,512]{1,0:T(8,128)(2,1)S(1)} %collective-permute-done.p1_ref.refs_1_), channel_id=1, source_target_pairs={{0,1},{1,0},{2,3},{3,2},{4,5},{5,4},{6,7},{7,6},{8,9},{9,8},{10,11... | collective-permute-start | bytes 1867784 | tf_op jit(solution)/shard_map/gather/ppermute | solution.py:348
  73.0 9.5 %collective-permute-start.5 = (bf16[608,512]{1,0:T(8,128)(2,1)S(1)}, bf16[608,512]{1,0:T(8,128)(2,1)S(1)}, u32[]{:S(2)}, u32[]{:S(2)}) collective-permute-start(bf16[608,512]{1,0:T(8,128)(2,1)S(1)} %collective-permute-done.1.p2_ref.refs_2_), channel_id=1, source_target_pairs={{0,1},{1,0},{2,3},{3,2},{4,5},{5,4},{6,7},{7,6},{8,9},{9,8},{10,11... | collective-permute-start | bytes 1867784 | tf_op jit(solution)/shard_map/gather/ppermute | solution.py:348
  79.7 3.9 %collective-permute-start.6 = (bf16[608,512]{1,0:T(8,128)(2,1)S(1)}, bf16[608,512]{1,0:T(8,128)(2,1)S(1)}, u32[]{:S(2)}, u32[]{:S(2)}) collective-permute-start(bf16[608,512]{1,0:T(8,128)(2,1)S(1)} %collective-permute-done.2.p3_ref.refs_3_), channel_id=1, source_target_pairs={{0,1},{1,0},{2,3},{3,2},{4,5},{5,4},{6,7},{7,6},{8,9},{9,8},{10,11... | collective-permute-start | bytes 1867784 | tf_op jit(solution)/shard_map/gather/ppermute | solution.py:348
  84.9 1.2 copy-start.3
  86.2 0.7 copy-start.5
  89.5 1.5 copy-start.2
  91.0 1.0 copy-start.4
  129.3 8.9 %copy-start = (f32[4,256,256]{2,1,0:T(8,128)S(1)}, f32[4,256,256]{2,1,0:T(8,128)}, u32[]{:S(2)}) copy-start(f32[4,256,256]{2,1,0:T(8,128)} %t_ref.1) | copy-start | bytes 3145732
  129.3 8.9 %copy-start.6 = (s32[3]{0:T(128)S(1)}, s32[3]{0:T(128)}, u32[]{:S(2)}) copy-start(s32[3]{0:T(128)} %pad_add_fusion.place_ref) | copy-start | bytes 40
  130.3 18.8 %all-to-all-start.4 = ((f16[8,16,1152]{2,1,0:T(8,128)(2,1)}), f16[8,16,1152]{2,1,0:T(8,128)(2,1)}, u32[]{:S(2)}, u32[]{:S(2)}) async-start(f16[8,16,1152]{2,1,0:T(8,128)(2,1)} %broadcast_in_dim.2), calls=%async_computation.5 | async-start | bytes 589824 | tf_op jit(solution)/shard_map/window/all_to_all | solution.py:19
Sparse Core Ops, SparseCore 0:
  11.8 45.4 all-gather.1
  92.2 39.3 reduce-scatter.1
